TPU v7x, 256 devices: a whole 4x4x8 slice. The times are simulated.
256 devices in a mesh: pb: 16 (over y_hi, z), ka: 16 (over x, y_lo, core).
Axes of the slice: x: 4, y: 4 (y_hi: 2, y_lo: 2; y = y_hi * 2 + y_lo), z: 8, core: 2. Of those that a mesh axis runs over, the one named last changes fastest.
Arguments:
- tokens: bfloat16 [16, 2048, 768], P('ka', 'pb'), may hold values from -6 to 6
- pair: bfloat16 [2048, 2048, 128], P('pb', 'ka'), may hold values from -500 to 500
- token_chain_index: int32 [2048], replicated, may hold values from 0 to 7, never falling along the last dimension, each value on 1 to 1024 neighbouring positions
- key_mask: int32 [2048], replicated, may hold values 0 or 1
- norm_gain: float32 [768], replicated, may hold values from 0.25 to 1.75
- pair_gain: float32 [128], replicated, may hold values from 0.1 to 1.9
- pair_proj: float32 [128, 16], replicated, may hold values from -0.140625 to 0.140625
- chain_gain: float32 [16], replicated, may hold values from -2 to 260
- w_qkvg: bfloat16 [768, 3072], replicated, may hold values from -0.21875 to 0.21875
- w_out: bfloat16 [768, 768], replicated, may hold values from -1.75 to 1.75
Outputs:
- update: bfloat16 [16, 2048, 768], P('ka', 'pb')
Inputs may be any that keep to these rules, and one draw needn't show every extreme that they name: `token_chain_index`: chain ids never fall along the tokens.
All inputs are finite; a program needn't handle non-finite values.
Results may differ from a plain program's by a relative error of at most 0.02.
Values may be sent and summed in bfloat16 or wider, within the bound.
No kernel may reach another device: no remote copies, remote signals or barrier semaphores. Data moves between devices by JAX's collectives and lax.ppermute only.
A program may use at most 128 MiB of HBM per device.

v0:
```python
import jax
import jax.numpy as jnp
from jax import lax
from jax.sharding import PartitionSpec as P

epsilon = 1e-05


def norm_rows(values, gain):
    values = values.astype(jnp.float32)
    center = jnp.mean(values, axis=-1, keepdims=True)
    spread = jnp.mean(jnp.square(values - center), axis=-1, keepdims=True)
    return (values - center) * lax.rsqrt(spread + epsilon) * gain


def pair_bias(pair_rows, pair_gain, pair_proj, chain_query, chain_keys, chain_gain):
    zhat = norm_rows(pair_rows, pair_gain)
    head_bias = jnp.einsum("qkc,ch->hqk", zhat, pair_proj, precision=lax.Precision.HIGHEST)
    same = (chain_query[:, None] == chain_keys[None, :]).astype(jnp.float32)
    return head_bias + chain_gain[:, None, None] * same[None]


def apply_attention(query_vectors, keys, values, bias, key_mask, heads):
    q_count = query_vectors.shape[0]
    k_count = keys.shape[0]
    width = query_vectors.shape[1]
    hdim = width // heads
    query_heads = query_vectors.reshape(q_count, heads, hdim)
    key_heads = keys.reshape(k_count, heads, hdim)
    value_heads = values.reshape(k_count, heads, hdim)
    scores = jnp.einsum("qhd,khd->hqk", query_heads, key_heads, preferred_element_type=jnp.float32)
    scores = scores * hdim ** (-0.5) + bias
    scores = jnp.where(key_mask[None, None, :] > 0, scores, jnp.float32(-1000000000.0))
    top = jnp.max(scores, axis=-1, keepdims=True)
    expo = jnp.exp(scores - top)
    total = jnp.sum(expo, axis=-1)
    summed = jnp.einsum(
        "hqk,khd->qhd", expo.astype(jnp.bfloat16), value_heads, preferred_element_type=jnp.float32
    )
    return (summed / jnp.transpose(total)[:, :, None]).reshape(q_count, width)


def body(
    tokens,
    pair,
    token_chain_index,
    key_mask,
    norm_gain,
    pair_gain,
    pair_proj,
    chain_gain,
    w_qkvg,
    w_out,
):
    width = tokens.shape[2]
    q_count = tokens.shape[1]
    k_count = pair.shape[1]
    heads = chain_gain.shape[0]
    normalized_input = norm_rows(tokens, norm_gain).astype(jnp.bfloat16)
    query_weight = w_qkvg[:, :width]
    w_pairs = w_qkvg[:, width : 3 * width]
    gate_weight = w_qkvg[:, 3 * width :]
    query_vectors = jnp.einsum(
        "fop,pu->fou", normalized_input, query_weight, preferred_element_type=jnp.float32
    ).astype(jnp.bfloat16)
    gate_values = jnp.einsum(
        "fop,pu->fou", normalized_input, gate_weight, preferred_element_type=jnp.float32
    ).astype(jnp.bfloat16)
    row_start = lax.axis_index("pb") * q_count
    col_start = lax.axis_index("ka") * k_count
    chain_query = lax.dynamic_slice_in_dim(token_chain_index, row_start, q_count)
    chain_keys = lax.dynamic_slice_in_dim(token_chain_index, col_start, k_count)
    bias = pair_bias(pair, pair_gain, pair_proj, chain_query, chain_keys, chain_gain)
    key_values = jnp.einsum(
        "fop,pu->fou",
        lax.all_gather(normalized_input, "pb", axis=1, tiled=True),
        w_pairs,
        preferred_element_type=jnp.float32,
    ).astype(jnp.bfloat16)
    bias_all = lax.all_gather(bias, "ka", axis=2, tiled=True)

    def one_sample(items):
        query_one, pairs_one = items
        return apply_attention(
            query_one, pairs_one[:, :width], pairs_one[:, width:], bias_all, key_mask, heads
        )

    attended = lax.map(one_sample, (query_vectors, key_values))
    hidden = (jax.nn.sigmoid(gate_values.astype(jnp.float32)) * attended).astype(jnp.bfloat16)
    return jnp.einsum("sqd,de->sqe", hidden, w_out, preferred_element_type=jnp.float32).astype(
        jnp.bfloat16
    )


def solution(mesh):
    in_specs = (P("ka", "pb", None), P("pb", "ka", None), P(), P(), P(), P(), P(), P(), P(), P())
    out_specs = P("ka", "pb", None)
    return jax.shard_map(body, mesh=mesh, in_specs=in_specs, out_specs=out_specs, check_vma=False)
```

profile of v0, /device:TPU:2, one launch (start us, length us, event | category | flops | bytes accessed | tf_op | source)
XLA Modules:
  0.0 250.3 jit_solution(10574960976641568531)
XLA Ops:
  6.5 1.1 convert_reduce_fusion.1
  7.7 1.1 fusion.60
  8.8 1.8 fusion.62
  10.6 0.0 all-gather.3.cloned.1.call-update
  10.7 0.0 all-gather.5.cloned.1.call-start
  10.7 0.9 fusion.70
  11.7 0.1 compare_convert_fusion
  11.7 3.6 %convert_reduce_fusion = f32[128,128]{1,0:T(8,128)S(1)} fusion(bf16[128,128,128]{2,1,0:T(8,128)(2,1)} %param.11), kind=kLoop, calls=%fused_computation.5 | loop fusion | flops 4177920 | bytes 4259840 | tf_op jit(solution)/shard_map/reduce_sum | solution.py:11
  15.4 4.8 %fusion.4 = f32[128,128]{1,0:T(8,128)S(1)} fusion(bf16[128,128,128]{2,1,0:T(8,128)(2,1)S(1)} %copy-done.1, f32[128,128]{1,0:T(8,128)S(1)} %broadcast_multiply_fusion), kind=kLoop, calls=%fused_computation.8 | loop fusion | flops 8372224 | bytes 4325376 | tf_op jit(solution)/shard_map/reduce_sum | solution.py:12
  20.2 0.0 copy-start.4
  20.2 9.9 %fusion.6 = f32[128,128,16]{1,2,0:T(8,128)S(1)} fusion(bf16[128,128,128]{2,1,0:T(8,128)(2,1)S(1)} %copy-done.1, f32[128]{0:T(128)S(1)} %copy-done.6, f32[128,128]{1,0:T(8,128)S(1)} %add_rsqrt_fusion, f32[128,128]{1,0:T(8,128)S(1)} %broadcast_multiply_fusion, f32[128,16]{0,1:T(8,128)S(1)} %copy-done.5), kind=kOutput, calls=%fused_computation.10 | convolution fusion | flops 411041792 | bytes 5382656 | tf_op jit(solution)/shard_map/qkc,ch->hqk/dot_general | solution.py:18
  30.2 0.0 copy-start.3
  30.2 1.3 bitcast_add_fusion
  31.5 0.0 all-gather.5.cloned.1.call-update
  31.5 1.6 fusion.47
  33.2 0.2 copy.13
  33.3 73.7 %all-gather.3.cloned.1.call-done = bf16[1,2048,768]{2,1,0:T(8,128)(2,1)} async-done(((bf16[1,128,768]{2,1,0:T(8,128)(2,1)}), bf16[1,2048,768]{2,1,0:T(8,128)(2,1)}) %all-gather.3.cloned.1.call-update) | async-done | bytes 3145744 | tf_op jit(solution)/shard_map/all_gather | solution.py:76
  107.0 7.5 %convolution_convert_fusion = bf16[2048,1536]{0,1:T(8,128)(2,1)S(1)} fusion(bf16[1,2048,768]{2,1,0:T(8,128)(2,1)} %all-gather.3.cloned.1.call-done, bf16[768,3072]{1,0:T(8,128)(2,1)} %param.18), kind=kOutput, calls=%fused_computation.13 | convolution fusion | flops 4834983936 | bytes 11796480 | tf_op jit(solution)/shard_map/fop,pu->fou/dot_general | solution.py:74
  114.5 3.2 %fusion.69 = (bf16[2048,768]{0,1:T(8,128)(2,1)}, bf16[2048,768]{0,1:T(8,128)(2,1)}) fusion(bf16[2048,1536]{0,1:T(8,128)(2,1)S(1)} %convolution_convert_fusion), kind=kLoop, calls=%fused_computation.55 | loop fusion | bytes 12582912 | tf_op jit(solution)/shard_map/while/body/eval_jaxpr/slice | solution.py:85
  117.8 89.2 %all-gather.5.cloned.1.call-done = f32[16,128,2048]{2,1,0:T(8,128)} async-done(((f32[16,128,128]{2,1,0:T(8,128)}), f32[16,128,2048]{2,1,0:T(8,128)}) %all-gather.5.cloned.1.call-update) | async-done | bytes 16777232 | tf_op jit(solution)/shard_map/all_gather | solution.py:80
  207.0 15.5 %fusion.71 = (f32[16,128]{1,0:T(8,128)S(1)}, f32[16,128,2048]{2,1,0:T(8,128)}) fusion(f32[16,128,2048]{2,1,0:T(8,128)} %all-gather.5.cloned.1.call-done, bf16[128,16,48]{0,2,1:T(8,128)(2,1)S(1)} %bitcast.31, bf16[2048,16,48]{0,2,1:T(8,128)(2,1)} %bitcast.30, pred[2048]{0:T(1024)(128)(4,1)S(1)} %broadcast_compare_fusion), kind=kOutput, calls=%fused_computation.57 | convolution fusion | flops 419428352 | bytes 36907008 | tf_op jit(solution)/shard_map/while/body/eval_jaxpr/qhd,khd->hqk/dot_general | solution.py:31
  222.5 8.1 %fusion = f32[16,128]{1,0:T(8,128)S(1)} fusion(f32[16,128,2048]{2,1,0:T(8,128)} %get-tuple-element.28, f32[16,128]{1,0:T(8,128)S(1)} %get-tuple-element.26), kind=kLoop, calls=%fused_computation.2 | loop fusion | flops 8386560 | bytes 16793600 | tf_op jit(solution)/shard_map/while/body/eval_jaxpr/reduce_sum | solution.py:36
  230.6 9.8 %fusion.55 = f32[128,16,48]{0,2,1:T(8,128)S(1)} fusion(bf16[2048,16,48]{0,2,1:T(8,128)(2,1)} %bitcast.29, f32[16,128,2048]{2,1,0:T(8,128)} %get-tuple-element.28, f32[16,128]{1,0:T(8,128)S(1)} %get-tuple-element.26, f32[128,16]{0,1:T(8,128)S(1)} %bitcast.33), kind=kOutput, calls=%fused_computation.36 | convolution fusion | flops 411140096 | bytes 20332544 | tf_op jit(solution)/shard_map/while/body/eval_jaxpr/hqk,khd->qhd/dot_general | solution.py:37
  240.5 3.0 %fusion.52 = bf16[1,128,768]{2,1,0:T(8,128)(2,1)} fusion(bf16[768,768]{1,0:T(8,128)(2,1)S(1)} %copy-done, f32[128,768]{0,1:T(8,128)S(1)} %bitcast.32, bf16[768,3072]{1,0:T(8,128)(2,1)} %param.18, bf16[1,128,768]{2,1,0:T(8,128)(2,1)S(1)} %copy-done.2), kind=kOutput, calls=%fused_computation.34 | convolution fusion | flops 302776320 | bytes 3145728 | tf_op jit(solution)/shard_map/sqd,de->sqe/dot_general | solution.py:90
  (18 shorter events, 0.1 us)
Async XLA Ops:
  6.5 233.9 %copy-start = (bf16[768,768]{1,0:T(8,128)(2,1)S(1)}, bf16[768,768]{1,0:T(8,128)(2,1)}, u32[]{:S(2)}) copy-start(bf16[768,768]{1,0:T(8,128)(2,1)} %param.19) | copy-start | bytes 3538948
  6.5 100.5 %all-gather.3.cloned.1.call-start = ((), (), s32[]{:S(2)}) async-start(), calls=%async_computation | async-start | bytes 3342336 | tf_op jit(solution)/shard_map/all_gather | solution.py:76
  8.8 11.4 %copy-start.5 = (f32[128,16]{0,1:T(8,128)S(1)}, f32[128,16]{0,1:T(8,128)}, u32[]{:S(2)}) copy-start(f32[128,16]{0,1:T(8,128)} %param.16) | copy-start | bytes 24580
  8.8 11.4 %copy-start.6 = (f32[128]{0:T(128)S(1)}, f32[128]{0:T(128)}, u32[]{:S(2)}) copy-start(f32[128]{0:T(128)} %param.15) | copy-start | bytes 1540
  10.7 196.3 %all-gather.5.cloned.1.call-start = ((), (), s32[]{:S(2)}) async-start(), calls=%async_computation.1 | async-start | bytes 17825792 | tf_op jit(solution)/shard_map/all_gather | solution.py:80
  10.7 4.7 %copy-start.1 = (bf16[128,128,128]{2,1,0:T(8,128)(2,1)S(1)}, bf16[128,128,128]{2,1,0:T(8,128)(2,1)}, u32[]{:S(2)}) copy-start(bf16[128,128,128]{2,1,0:T(8,128)(2,1)} %param.11) | copy-start | bytes 12582916
  20.2 10.0 %copy-start.4 = (f32[16]{0:T(128)S(1)}, f32[16]{0:T(128)}, u32[]{:S(2)}) copy-start(f32[16]{0:T(128)} %param.17) | copy-start | bytes 196
  20.2 11.3 %copy-start.2 = (bf16[1,128,768]{2,1,0:T(8,128)(2,1)S(1)}, bf16[1,128,768]{2,1,0:T(8,128)(2,1)}, u32[]{:S(2)}) copy-start(bf16[1,128,768]{2,1,0:T(8,128)(2,1)} %fusion.62) | copy-start | bytes 589828
  30.2 3.2 %copy-start.3 = (s32[2048]{0:T(1024)S(1)}, s32[2048]{0:T(1024)}, u32[]{:S(2)}) copy-start(s32[2048]{0:T(1024)} %param.13) | copy-start | bytes 24580
Sparse Core Ops, SparseCore 0:
  10.8 96.2 all-gather.2
  108.8 98.1 all-gather.4
where the time goes:
time: 252 us; the launch traced here: 250 us
  waiting for transfers between devices  163 us (65%)
  matrix products  47.3 us (19%)
  other arithmetic  22 us (9%)
  between operations  13.6 us (5%)
  local copies, waits for them, and re-layouts  4.38 us (2%)
    all_gather x1, waiting for transfers between devices, body(): bias_all = lax.all_gather(bias, 'ka', axis=2, tiled=True)  89.2 us
    all_gather x1, waiting for transfers between devices, body(): lax.all_gather(normalized_input, 'pb', axis=1, tiled=True)  73.7 us
    dot_general x1, matrix products, apply_attention(): jnp.einsum('qhd,khd->hqk', query_heads, key_heads, preferred_element_type...  15.5 us
    dot_general x1, matrix products, pair_bias(): jnp.einsum('qkc,ch->hqk', zhat, pair_proj, precision=lax.Precision.HIGHEST)  9.91 us
    dot_general x1, matrix products, apply_attention(): jnp.einsum('hqk,khd->qhd', expo.astype(jnp.bfloat16), value_heads, prefer...  9.84 us
    reduce_sum x1, other arithmetic, apply_attention(): total = jnp.sum(expo, axis=-1)  8.14 us
    dot_general x1, matrix products, body(): jnp.einsum('fop,pu->fou', lax.all_gather(normalized_input, 'pb', axis=1,...  7.49 us
    reduce_sum x2, other arithmetic, norm_rows(): spread = jnp.mean(jnp.square(values - center), axis=-1, keepdims=True)  5.9 us
  transfers between devices with their start and end apart: 2, of which 2 were waited for; matrix products, arithmetic and copies ran while one was open for 13% of the time, Pallas kernels for 0%

commit v1 on v0

v1 whole, which is shorter than its diff:
```python
import functools
import math

import jax
import jax.numpy as jnp
from jax import lax
from jax.experimental import pallas as pl
from jax.experimental.pallas import tpu as pltpu
from jax.sharding import PartitionSpec as P

EPS = 1e-05
LOG2E = 1.4426950408889634
NEG = -1000000000.0 * LOG2E
F32 = jnp.float32
BF16 = jnp.bfloat16
MIB = 1024 * 1024


def dot(a, b, dims):
    return lax.dot_general(a, b, (dims, ((), ())), preferred_element_type=F32)


def params(mib):
    return pltpu.CompilerParams(vmem_limit_bytes=mib * MIB)


def norm_kernel(x_ref, gain_ref, out_ref):
    x = x_ref[...].astype(F32)
    center = jnp.mean(x, axis=-1, keepdims=True)
    d = x - center
    spread = jnp.mean(d * d, axis=-1, keepdims=True)
    out_ref[...] = (d * lax.rsqrt(spread + EPS) * gain_ref[...]).astype(BF16)


def norm_rows(x, gain):
    return pl.pallas_call(
        norm_kernel,
        out_shape=jax.ShapeDtypeStruct(x.shape, BF16),
        compiler_params=params(16),
    )(x, gain.reshape(1, -1))


def bias_kernel(pair_ref, gain_ref, proj_ref, out_ref, w_ref, swap_ref):
    nq, nk, nc = pair_ref.shape
    heads = out_ref.shape[0]

    @pl.when(pl.program_id(0) == 0)
    def _():
        w = proj_ref[...] * gain_ref[...] * LOG2E
        w = w - jnp.mean(w, axis=-1, keepdims=True)
        hi = w.astype(BF16)
        rest = w - hi.astype(F32)
        mid = rest.astype(BF16)
        low = (rest - mid.astype(F32)).astype(BF16)
        w_ref[...] = jnp.concatenate([hi, mid, low], axis=0)

    x = pair_ref[...].reshape(nq * nk, nc)
    ones = jnp.full((nc, nc), 1.0 / nc, BF16)
    center = dot(x, ones, ((1,), (0,)))
    d = x.astype(F32) - center
    d = d * d
    hi = d.astype(BF16)
    low = (d - hi.astype(F32)).astype(BF16)
    parts = jnp.concatenate([hi, low], axis=1)
    spread = dot(jnp.full((8, 2 * nc), 1.0 / nc, BF16), parts, ((1,), (1,)))[:1]
    r = dot(w_ref[...], x, ((1,), (1,)))
    r = r[:heads] + r[heads : 2 * heads] + r[2 * heads :]
    r = r * lax.rsqrt(spread + EPS)
    for q in range(nq):
        swap_ref[pl.ds(q, heads, stride=nq), :] = r[:, q * nk : (q + 1) * nk]
    out_ref[...] = swap_ref[...].reshape(heads, nq, nk).astype(BF16)


def pair_bias(pair, gain, proj_t, first, rows):
    nk, nc = pair.shape[1:]
    heads = proj_t.shape[0]
    step = 16
    return pl.pallas_call(
        bias_kernel,
        grid=(rows // step,),
        in_specs=[
            pl.BlockSpec((step, nk, nc), lambda i: (first // step + i, 0, 0)),
            pl.BlockSpec((1, nc), lambda i: (0, 0)),
            pl.BlockSpec((heads, nc), lambda i: (0, 0)),
        ],
        out_specs=pl.BlockSpec((heads, step, nk), lambda i: (0, i, 0)),
        out_shape=jax.ShapeDtypeStruct((heads, rows, nk), BF16),
        scratch_shapes=[pltpu.VMEM((3 * heads, nc), BF16), pltpu.VMEM((heads * step, nk), F32)],
        compiler_params=params(32),
        cost_estimate=pl.CostEstimate(
            flops=rows * nk * nc * 400, bytes_accessed=rows * nk * nc * 2, transcendentals=0
        ),
    )(pair, gain.reshape(1, -1), proj_t)


def kv_kernel(pos_ref, w_ref, *refs):
    blocks, out_ref = refs[:-1], refs[-1]
    rows = 256
    n = blocks[0].shape[0]
    for i in range(0, len(blocks), 2):
        x = jnp.concatenate([blocks[i][...], blocks[i + 1][...]], axis=0)
        at = [pl.multiple_of(pos_ref[i + j] * n, n) for j in range(2)]

        def one(m, _):
            m0 = pl.multiple_of(m * rows, rows)
            y = dot(w_ref[pl.ds(m0, rows), :], x, ((1,), (1,))).astype(BF16)
            for j in range(2):
                out_ref[pl.ds(m0, rows), pl.ds(at[j], n)] = y[:, j * n : (j + 1) * n]
            return 0

        lax.fori_loop(0, w_ref.shape[0] // rows, one, 0, unroll=True)


def keys_values(pos, w_t, blocks):
    n = blocks[0].shape[0]
    out = (w_t.shape[0], n * len(blocks))
    vmem = pl.BlockSpec(memory_space=pltpu.VMEM)
    return pl.pallas_call(
        kv_kernel,
        in_specs=[pl.BlockSpec(memory_space=pltpu.SMEM)] + [vmem] * (1 + len(blocks)),
        out_specs=vmem,
        out_shape=jax.ShapeDtypeStruct(out, BF16),
        compiler_params=params(40),
        cost_estimate=pl.CostEstimate(
            flops=2 * w_t.shape[0] * w_t.shape[1] * out[1], bytes_accessed=12 * MIB, transcendentals=0
        ),
    )(pos, w_t, *blocks)


def attend_kernel(scale, per, q_ref, k_ref, v_ref, bias_ref, chain_ref, mask_ref, gate_ref, w_ref, out_ref, hid_ref):
    step = pl.program_id(0)
    hdim = k_ref.shape[0] // per
    blocks = bias_ref.shape[0]
    for h in range(per):
        k = jnp.concatenate([k_ref[h * hdim : (h + 1) * hdim, :], chain_ref[...]], axis=0)
        s = dot(q_ref[h], k, ((1,), (0,))) * scale
        s = s + jnp.concatenate([bias_ref[c, h].astype(F32) for c in range(blocks)], axis=1)
        s = jnp.minimum(s, mask_ref[...])
        top = jnp.max(s, axis=-1, keepdims=True)
        p = jnp.exp2(s - top)
        total = jnp.sum(p, axis=-1, keepdims=True)
        o = dot(p.astype(BF16), v_ref[h * hdim : (h + 1) * hdim, :], ((1,), (1,)))
        o = o / total
        row = pl.multiple_of(step * (per * hdim) + h * hdim, 16)
        gate = gate_ref[pl.ds(row, hdim), :].astype(F32)
        hid_ref[pl.ds(row, hdim), :] = (jax.nn.sigmoid(gate) * o.T).astype(BF16)

    @pl.when(step == pl.num_programs(0) - 1)
    def _():
        out_ref[...] = dot(hid_ref[...], w_ref[...], ((0,), (0,))).astype(BF16)


def attend(q_aug, kv, bias, chain_rows, mask_row, gates_t, w_out):
    heads, nq, depth = q_aug.shape
    width = w_out.shape[0]
    hdim = width // heads
    keys = kv.shape[1]
    per = 4
    steps = heads // per
    scale = hdim**-0.5 * LOG2E
    whole = lambda *s: pl.BlockSpec(s, lambda i: (0,) * len(s))
    return pl.pallas_call(
        functools.partial(attend_kernel, scale, per),
        grid=(steps,),
        in_specs=[
            pl.BlockSpec((per, nq, depth), lambda i: (i, 0, 0)),
            pl.BlockSpec((per * hdim, keys), lambda i: (i, 0)),
            pl.BlockSpec((per * hdim, keys), lambda i: (i + steps, 0)),
            pl.BlockSpec((bias.shape[0], per, nq, bias.shape[3]), lambda i: (0, i, 0, 0)),
            whole(*chain_rows.shape),
            whole(*mask_row.shape),
            whole(*gates_t.shape),
            whole(*w_out.shape),
        ],
        out_specs=whole(nq, width),
        out_shape=jax.ShapeDtypeStruct((nq, width), BF16),
        scratch_shapes=[pltpu.VMEM((width, nq), BF16)],
        compiler_params=params(48),
        cost_estimate=pl.CostEstimate(
            flops=heads * nq * keys * 1024, bytes_accessed=heads * nq * keys * 2, transcendentals=heads * nq * keys
        ),
    )(q_aug, kv, kv, bias, chain_rows, mask_row, gates_t, w_out)


def shift_z(x, by):
    def to(i):
        return (i // 8) * 8 + (i % 8 + by) % 8

    return lax.ppermute(x, "pb", [(i, to(i)) for i in range(16)])


def swap_y(x):
    return lax.ppermute(x, "pb", [(i, (i + 8) % 16) for i in range(16)])


def gather_rows(own):
    me = lax.axis_index("pb")
    y, z = me // 8, me % 8
    other = swap_y(own)
    blocks, places = [own, other], [me, (1 - y) * 8 + z]
    for start, row, last in ((own, y, 1), (other, 1 - y, -1)):
        for by in (1, -1):
            now = start
            for hop in range(1, 5 if by == last else 4):
                now = shift_z(now, by)
                blocks.append(now)
                places.append(row * 8 + (z - by * hop) % 8)
    return blocks, jnp.stack(places).astype(jnp.int32)


def body(tokens, pair, token_chain_index, key_mask, norm_gain, pair_gain, pair_proj, chain_gain, w_qkvg, w_out):
    nq, width = tokens.shape[1:]
    heads = chain_gain.shape[0]
    hdim = width // heads
    keys = token_chain_index.shape[0]

    normed = norm_rows(tokens[0], norm_gain)
    proj_t = pair_proj.T
    half = nq // 2
    parts = [pair_bias(pair, pair_gain, proj_t, i * half, half) for i in range(2)]
    full = [lax.all_gather(b, "ka", axis=0, tiled=False) for b in parts]
    blocks, places = gather_rows(normed)

    w_t = w_qkvg.T
    kv = keys_values(places, w_t[width : 3 * width], blocks)

    q = dot(normed, w_qkvg[:, :width], ((1,), (0,))).astype(BF16)
    q = q.reshape(nq, heads, hdim).transpose(1, 0, 2)
    chain_query = lax.dynamic_slice_in_dim(token_chain_index, lax.axis_index("pb") * nq, nq)
    kinds = jnp.arange(8, dtype=jnp.int32)
    gain = chain_gain * math.sqrt(hdim)
    hi = gain.astype(BF16)
    rest = gain - hi.astype(F32)
    mid = rest.astype(BF16)
    low = (rest - mid.astype(F32)).astype(BF16)
    gains = jnp.stack([hi, mid, low, jnp.zeros_like(hi)], axis=1)
    hot_q = (chain_query[:, None] == kinds[None, :]).astype(BF16)
    chain_q = (gains[:, None, :, None] * hot_q[None, :, None, :]).reshape(heads, nq, 32)
    q_aug = jnp.concatenate([q, chain_q], axis=2)
    hot_k = (token_chain_index[None, :] == kinds[:, None]).astype(BF16)
    chain_rows = jnp.concatenate([hot_k] * 4, axis=0)
    mask_row = jnp.where(key_mask > 0, F32(3.0e38), F32(NEG)).reshape(1, keys)
    gates_t = dot(w_t[3 * width :], normed, ((1,), (1,))).astype(BF16)

    out = [
        attend(
            q_aug[:, i * half : (i + 1) * half],
            kv,
            full[i],
            chain_rows,
            mask_row,
            gates_t[:, i * half : (i + 1) * half],
            w_out,
        )
        for i in range(2)
    ]
    return jnp.concatenate(out, axis=0)[None]


def solution(mesh):
    in_specs = (P("ka", "pb", None), P("pb", "ka", None), P(), P(), P(), P(), P(), P(), P(), P())
    out_specs = P("ka", "pb", None)
    return jax.shard_map(body, mesh=mesh, in_specs=in_specs, out_specs=out_specs, check_vma=False)
```

time: 252 us -> 123 us (0.49)
  waiting for transfers between devices: 163 us -> 13.8 us
  matrix products: 47.3 us -> 3.38 us
  Pallas kernels: 0 us -> 30.1 us
  local copies, waits for them, and re-layouts: 4.38 us -> 31 us
  starting transfers between devices: 0.04 us -> 23.1 us
  other arithmetic: 22 us -> 6.8 us
    all_gather x2, waiting for transfers between devices: 163 us -> 0.02 us  [body(): full = [lax.all_gather(b, 'ka', axis=0, tiled=False) for b in parts]]
    dot_general x6 -> x2, matrix products: 47.3 us -> 3.38 us  [dot(): return lax.dot_general(a, b, (dims, ((), ())), preferred_element_type=F32)]
    pallas_call x0 -> x6, Pallas kernels: none -> 30.1 us  [the longest x2 14.9 us: attend(): pl.pallas_call(functools.partial(attend_kernel, scale, per), grid=(steps,...]
    unnamed x14 -> x57, local copies, waits for them, and re-layouts: 0.04 us -> 26.7 us
    ppermute x0 -> x15, starting transfers between devices: none -> 23 us  [the longest x14 19.8 us: shift_z(): return lax.ppermute(x, 'pb', [(i, to(i)) for i in range(16)])]
    reduce_sum x5 -> x0, other arithmetic: 18.8 us -> none  [the longest x1 8.14 us: apply_attention(): total = jnp.sum(expo, axis=-1)]
    ppermute x0 -> x15, waiting for transfers between devices: none -> 13.7 us  [the longest x14 13.7 us: shift_z(): return lax.ppermute(x, 'pb', [(i, to(i)) for i in range(16)])]
    concatenate x0 -> x2, other arithmetic: none -> 3.84 us  [the longest x1 2.33 us: body(): q_aug = jnp.concatenate([q, chain_q], axis=2)]
  transfers between devices with their start and end apart: 2 -> 17, of which waited for: 2 -> 5; matrix products, arithmetic and copies ran while one was open for 13% -> 17% of each run, Pallas kernels for 0% -> 15%
where the time goes in v1:
time: 123 us; the launch traced here: 122 us
  local copies, waits for them, and re-layouts  31 us (25%)
  Pallas kernels  30.1 us (24%)
  starting transfers between devices  23.1 us (19%)
  waiting for transfers between devices  13.8 us (11%)
  between operations  13.7 us (11%)
  other arithmetic  6.8 us (6%)
  matrix products  3.38 us (3%)
    unnamed x57, local copies, waits for them, and re-layouts  26.7 us
    ppermute x14, starting transfers between devices, shift_z(): return lax.ppermute(x, 'pb', [(i, to(i)) for i in range(16)])  19.8 us
    pallas_call x2, Pallas kernels, attend(): pl.pallas_call(functools.partial(attend_kernel, scale, per), grid=(steps,...  14.9 us
    ppermute x14, waiting for transfers between devices, shift_z(): return lax.ppermute(x, 'pb', [(i, to(i)) for i in range(16)])  13.7 us
    pallas_call x2, Pallas kernels, pair_bias(): pl.pallas_call(bias_kernel, grid=(rows // step,), in_specs=[pl.BlockSpec(...  7.99 us
    pallas_call x1, Pallas kernels, keys_values(): pl.pallas_call(kv_kernel, in_specs=[pl.BlockSpec(memory_space=pltpu.SMEM)...  6.94 us
    dot_general x2, matrix products, dot(): return lax.dot_general(a, b, (dims, ((), ())), preferred_element_type=F32)  3.38 us
    ppermute x1, starting transfers between devices, swap_y(): return lax.ppermute(x, 'pb', [(i, (i + 8) % 16) for i in range(16)])  3.28 us
  transfers between devices with their start and end apart: 17, of which 5 were waited for; matrix products, arithmetic and copies ran while one was open for 17% of the time, Pallas kernels for 15%

profile of v1, /device:TPU:2, one launch (start us, length us, event | category | flops | bytes accessed | tf_op | source)
XLA Modules:
  0.0 121.8 jit_solution(14628299675109718807)
XLA Ops:
  6.5 2.2 %copy-done.1 = bf16[128,128,128]{2,1,0:T(8,128)(2,1)S(1)} copy-done((bf16[128,128,128]{2,1,0:T(8,128)(2,1)S(1)}, bf16[128,128,128]{2,1,0:T(8,128)(2,1)}, u32[]{:S(2)}) %copy-start.1) | copy-done | bytes 4194328
  10.1 4.0 %shard_map.102 = bf16[16,64,128]{2,1,0:T(8,128)(2,1)} custom-call(bf16[128,128,128]{2,1,0:T(8,128)(2,1)S(1)} %copy-done.1, f32[1,128]{1,0:T(1,128)S(1)} %bitcast.49, f32[16,128]{1,0:T(8,128)S(1)} %bitcast.47), custom_call_target="tpu_custom_call" | custom-call | flops 419430400 | bytes 2097152 | tf_op jit(solution)/shard_map/pallas_call | solution.py:78
  14.2 2.2 %copy-done.2 = bf16[128,128,128]{2,1,0:T(8,128)(2,1)S(1)} copy-done((bf16[128,128,128]{2,1,0:T(8,128)(2,1)S(1)}, bf16[128,128,128]{2,1,0:T(8,128)(2,1)}, u32[]{:S(2)}) %copy-start.2) | copy-done | bytes 4194328
  16.4 4.0 %shard_map.104 = bf16[16,64,128]{2,1,0:T(8,128)(2,1)} custom-call(bf16[128,128,128]{2,1,0:T(8,128)(2,1)S(1)} %copy-done.2, f32[1,128]{1,0:T(1,128)S(1)} %bitcast.50, f32[16,128]{1,0:T(8,128)S(1)} %bitcast.48), custom_call_target="tpu_custom_call" | custom-call | flops 419430400 | bytes 2097152 | tf_op jit(solution)/shard_map/pallas_call | solution.py:78
  20.7 3.3 %collective-permute-start = (bf16[128,768]{1,0:T(8,128)(2,1)S(1)}, bf16[128,768]{1,0:T(8,128)(2,1)S(1)}, u32[]{:S(2)}, u32[]{:S(2)}) collective-permute-start(bf16[128,768]{1,0:T(8,128)(2,1)S(1)} %shard_map.100.refs_0_), channel_id=1, source_target_pairs={{0,128},{16,144},{32,160},{48,176},{64,192},{80,208},{96,224},{112... | collective-permute-start | bytes 589832 | tf_op jit(solution)/shard_map/ppermute | solution.py:193
  25.9 3.9 %collective-permute-start.5 = (bf16[128,768]{1,0:T(8,128)(2,1)S(1)}, bf16[128,768]{1,0:T(8,128)(2,1)S(1)}, u32[]{:S(2)}, u32[]{:S(2)}) collective-permute-start(bf16[128,768]{1,0:T(8,128)(2,1)S(1)} %shard_map.100.refs_0_), channel_id=1, source_target_pairs={{0,112},{16,0},{32,16},{48,32},{64,48},{80,64},{96,80},{112,96},{1... | collective-permute-start | bytes 589832 | tf_op jit(solution)/shard_map/ppermute | solution.py:189
  33.4 6.7 %copy.24 = bf16[768,3072]{0,1:T(8,128)(2,1)} copy(bf16[768,3072]{1,0:T(8,128)(2,1)} %param.18) | data formatting | bytes 9437184 | tf_op args[8]
  43.2 2.3 %fusion.13 = (bf16[16,64,80]{2,1,0:T(8,128)(2,1)}, bf16[16,64,80]{2,1,0:T(8,128)(2,1)}) fusion(bf16[16,128,48]{2,1,0:T(8,128)(2,1)} %bitcast.53, bf16[16,128,32]{2,1,0:T(8,128)(2,1)} %broadcast_multiply_fusion), kind=kLoop, calls=%fused_computation.9 | loop fusion | flops 655360 | bytes 655360 | tf_op jit(solution)/shard_map/concatenate | solution.py:239
  45.5 2.1 %collective-permute-start.11 = (bf16[128,768]{1,0:T(8,128)(2,1)S(1)}, bf16[128,768]{1,0:T(8,128)(2,1)S(1)}, u32[]{:S(2)}, u32[]{:S(2)}) collective-permute-start(bf16[128,768]{1,0:T(8,128)(2,1)S(1)} %collective-permute-done.refs_1_), channel_id=1, source_target_pairs={{0,112},{16,0},{32,16},{48,32},{64,48},{80,64},{96,80},{112,96},{1... | collective-permute-start | bytes 589832 | tf_op jit(solution)/shard_map/ppermute | solution.py:189
  49.6 2.0 %collective-permute-done.11.refs_12_ = bf16[128,768]{1,0:T(8,128)(2,1)S(1)} collective-permute-done((bf16[128,768]{1,0:T(8,128)(2,1)S(1)}, bf16[128,768]{1,0:T(8,128)(2,1)S(1)}, u32[]{:S(2)}, u32[]{:S(2)}) %collective-permute-start.11) | collective-permute-done | bytes 196640 | tf_op jit(solution)/shard_map/ppermute | solution.py:189
  51.7 3.0 %collective-permute-start.12 = (bf16[128,768]{1,0:T(8,128)(2,1)S(1)}, bf16[128,768]{1,0:T(8,128)(2,1)S(1)}, u32[]{:S(2)}, u32[]{:S(2)}) collective-permute-start(bf16[128,768]{1,0:T(8,128)(2,1)S(1)} %collective-permute-done.11.refs_12_), channel_id=1, source_target_pairs={{0,112},{16,0},{32,16},{48,32},{64,48},{80,64},{96,80},{112,96},{1... | collective-permute-start | bytes 589832 | tf_op jit(solution)/shard_map/ppermute | solution.py:189
  56.3 2.3 %collective-permute-done.8.refs_9_ = bf16[128,768]{1,0:T(8,128)(2,1)S(1)} collective-permute-done((bf16[128,768]{1,0:T(8,128)(2,1)S(1)}, bf16[128,768]{1,0:T(8,128)(2,1)S(1)}, u32[]{:S(2)}, u32[]{:S(2)}) %collective-permute-start.8) | collective-permute-done | bytes 196640 | tf_op jit(solution)/shard_map/ppermute | solution.py:189
  58.6 4.2 %collective-permute-done.2.refs_3_ = bf16[128,768]{1,0:T(8,128)(2,1)S(1)} collective-permute-done((bf16[128,768]{1,0:T(8,128)(2,1)S(1)}, bf16[128,768]{1,0:T(8,128)(2,1)S(1)}, u32[]{:S(2)}, u32[]{:S(2)}) %collective-permute-start.2) | collective-permute-done | bytes 196640 | tf_op jit(solution)/shard_map/ppermute | solution.py:189
  62.8 3.2 %collective-permute-start.13 = (bf16[128,768]{1,0:T(8,128)(2,1)S(1)}, bf16[128,768]{1,0:T(8,128)(2,1)S(1)}, u32[]{:S(2)}, u32[]{:S(2)}) collective-permute-start(bf16[128,768]{1,0:T(8,128)(2,1)S(1)} %collective-permute-done.12.refs_13_), channel_id=1, source_target_pairs={{0,112},{16,0},{32,16},{48,32},{64,48},{80,64},{96,80},{112,96},{1... | collective-permute-start | bytes 589832 | tf_op jit(solution)/shard_map/ppermute | solution.py:189
  67.6 2.0 %collective-permute-start.10 = (bf16[128,768]{1,0:T(8,128)(2,1)S(1)}, bf16[128,768]{1,0:T(8,128)(2,1)S(1)}, u32[]{:S(2)}, u32[]{:S(2)}) collective-permute-start(bf16[128,768]{1,0:T(8,128)(2,1)S(1)} %collective-permute-done.9.refs_10_), channel_id=1, source_target_pairs={{0,16},{16,32},{32,48},{48,64},{64,80},{80,96},{96,112},{112,0},{1... | collective-permute-start | bytes 589832 | tf_op jit(solution)/shard_map/ppermute | solution.py:189
  69.6 2.3 %collective-permute-done.3.refs_4_ = bf16[128,768]{1,0:T(8,128)(2,1)S(1)} collective-permute-done((bf16[128,768]{1,0:T(8,128)(2,1)S(1)}, bf16[128,768]{1,0:T(8,128)(2,1)S(1)}, u32[]{:S(2)}, u32[]{:S(2)}) %collective-permute-start.3) | collective-permute-done | bytes 196640 | tf_op jit(solution)/shard_map/ppermute | solution.py:189
  71.8 3.2 %collective-permute-start.14 = (bf16[128,768]{1,0:T(8,128)(2,1)S(1)}, bf16[128,768]{1,0:T(8,128)(2,1)S(1)}, u32[]{:S(2)}, u32[]{:S(2)}) collective-permute-start(bf16[128,768]{1,0:T(8,128)(2,1)S(1)} %collective-permute-done.13.refs_14_), channel_id=1, source_target_pairs={{0,112},{16,0},{32,16},{48,32},{64,48},{80,64},{96,80},{112,96},{1... | collective-permute-start | bytes 589832 | tf_op jit(solution)/shard_map/ppermute | solution.py:189
  75.8 2.9 %collective-permute-done.4.refs_5_ = bf16[128,768]{1,0:T(8,128)(2,1)S(1)} collective-permute-done((bf16[128,768]{1,0:T(8,128)(2,1)S(1)}, bf16[128,768]{1,0:T(8,128)(2,1)S(1)}, u32[]{:S(2)}, u32[]{:S(2)}) %collective-permute-start.4) | collective-permute-done | bytes 196640 | tf_op jit(solution)/shard_map/ppermute | solution.py:189
  82.4 6.9 %shard_map.101.k_ref.v_ref = bf16[1536,2048]{1,0:T(8,128)(2,1)S(1)} custom-call(s32[16]{0:T(128)S(1)} %stack.83.pos_ref, bf16[1536,768]{1,0:T(8,128)(2,1)S(1)} %slice.30.w_ref, bf16[128,768]{1,0:T(8,128)(2,1)S(1)} %copy-done.14, bf16[128,768]{1,0:T(8,128)(2,1)S(1)} %copy-done.20, bf16[128,768]{1,0:T(8,128)(2,1)S(1)} %copy-done.22, ...), custom_call_target="tpu_custom_call" | custom-call | flops 4831838208 | bytes 12582912 | tf_op jit(solution)/shard_map/pallas_call | solution.py:118
  89.4 2.7 %copy-done = bf16[1536,2048]{1,0:T(8,128)(2,1)} copy-done((bf16[1536,2048]{1,0:T(8,128)(2,1)}, bf16[1536,2048]{1,0:T(8,128)(2,1)S(1)}, u32[]{:S(2)}) %copy-start) | copy-done | bytes 6291480
  92.1 2.3 %copy-done.4 = bf16[256,64,128]{2,1,0:T(8,128)(2,1)S(1)} copy-done((bf16[256,64,128]{2,1,0:T(8,128)(2,1)S(1)}, bf16[256,64,128]{2,1,0:T(8,128)(2,1)}, u32[]{:S(2)}) %copy-start.4) | copy-done | bytes 4194328
  97.1 7.5 %shard_map.103 = bf16[64,768]{1,0:T(8,128)(2,1)S(1)} custom-call(bf16[16,64,80]{2,1,0:T(8,128)(2,1)S(1)} %copy-done.9, bf16[1536,2048]{1,0:T(8,128)(2,1)} %copy-done, bf16[1536,2048]{1,0:T(8,128)(2,1)} %copy-done, bf16[16,16,64,128]{3,2,1,0:T(8,128)(2,1)S(1)} %bitcast.42, bf16[32,2048]{1,0:T(8,128)(2,1)S(1)} %copy-done.6, f32[1,2048]{1,0:T(1,128)S(1)} %bitcast.45, ...), custom_call_target="tpu_custom_call" | custom-call | flops 2147483648 | bytes 4194304 | tf_op jit(solution)/shard_map/pallas_call | solution.py:162
  104.7 2.2 %copy-done.5 = bf16[256,64,128]{2,1,0:T(8,128)(2,1)S(1)} copy-done((bf16[256,64,128]{2,1,0:T(8,128)(2,1)S(1)}, bf16[256,64,128]{2,1,0:T(8,128)(2,1)}, u32[]{:S(2)}) %copy-start.5) | copy-done | bytes 4194328
  106.9 7.4 %shard_map.105 = bf16[64,768]{1,0:T(8,128)(2,1)S(1)} custom-call(bf16[16,64,80]{2,1,0:T(8,128)(2,1)S(1)} %copy-done.8, bf16[1536,2048]{1,0:T(8,128)(2,1)} %copy-done, bf16[1536,2048]{1,0:T(8,128)(2,1)} %copy-done, bf16[16,16,64,128]{3,2,1,0:T(8,128)(2,1)S(1)} %bitcast.43, bf16[32,2048]{1,0:T(8,128)(2,1)S(1)} %copy-done.7, f32[1,2048]{1,0:T(1,128)S(1)} %bitcast.46, ...), custom_call_target="tpu_custom_call" | custom-call | flops 2147483648 | bytes 4194304 | tf_op jit(solution)/shard_map/pallas_call | solution.py:162
  (98 shorter events, 23.4 us)
Async XLA Ops:
  6.5 85.5 %all-gather.5.cloned.1.call-start = ((), (), s32[]{:S(2)}) async-start(), calls=%async_computation | async-start | bytes 4456448 | tf_op jit(solution)/shard_map/all_gather | solution.py:221
  10.1 10.3 %copy-start.12 = (bf16[1,128,768]{2,1,0:T(8,128)(2,1)S(1)}, bf16[1,128,768]{2,1,0:T(8,128)(2,1)}, u32[]{:S(2)}) copy-start(bf16[1,128,768]{2,1,0:T(8,128)(2,1)} %param.10) | copy-start | bytes 589828
  10.1 19.7 %copy-start.25 = (s32[2048]{0:T(1024)S(1)}, s32[2048]{0:T(1024)}, u32[]{:S(2)}) copy-start(s32[2048]{0:T(1024)} %param.12) | copy-start | bytes 24580
  10.1 20.0 %copy-start.27 = (f32[16]{0:T(128)S(1)}, f32[16]{0:T(128)}, u32[]{:S(2)}) copy-start(f32[16]{0:T(128)} %param.17) | copy-start | bytes 196
  14.1 90.5 %all-gather.7.cloned.1.call-start = ((), (), s32[]{:S(2)}) async-start(), calls=%async_computation.1 | async-start | bytes 4456448 | tf_op jit(solution)/shard_map/all_gather | solution.py:221
  20.7 27.0 %copy-start.13 = (bf16[128,768]{1,0:T(8,128)(2,1)}, bf16[128,768]{1,0:T(8,128)(2,1)S(1)}, u32[]{:S(2)}) copy-start(bf16[128,768]{1,0:T(8,128)(2,1)S(1)} %shard_map.100.refs_0_) | copy-start | bytes 589828
  20.7 24.9 %collective-permute-start = (bf16[128,768]{1,0:T(8,128)(2,1)S(1)}, bf16[128,768]{1,0:T(8,128)(2,1)S(1)}, u32[]{:S(2)}, u32[]{:S(2)}) collective-permute-start(bf16[128,768]{1,0:T(8,128)(2,1)S(1)} %shard_map.100.refs_0_), channel_id=1, source_target_pairs={{0,128},{16,144},{32,160},{48,176},{64,192},{80,208},{96,224},{112... | collective-permute-start | bytes 589832 | tf_op jit(solution)/shard_map/ppermute | solution.py:193
  24.0 25.6 %collective-permute-start.1 = (bf16[128,768]{1,0:T(8,128)(2,1)S(1)}, bf16[128,768]{1,0:T(8,128)(2,1)S(1)}, u32[]{:S(2)}, u32[]{:S(2)}) collective-permute-start(bf16[128,768]{1,0:T(8,128)(2,1)S(1)} %shard_map.100.refs_0_), channel_id=1, source_target_pairs={{0,16},{16,32},{32,48},{48,64},{64,80},{80,96},{96,112},{112,0},{1... | collective-permute-start | bytes 589832 | tf_op jit(solution)/shard_map/ppermute | solution.py:189
  25.9 29.6 %collective-permute-start.5 = (bf16[128,768]{1,0:T(8,128)(2,1)S(1)}, bf16[128,768]{1,0:T(8,128)(2,1)S(1)}, u32[]{:S(2)}, u32[]{:S(2)}) collective-permute-start(bf16[128,768]{1,0:T(8,128)(2,1)S(1)} %shard_map.100.refs_0_), channel_id=1, source_target_pairs={{0,112},{16,0},{32,16},{48,32},{64,48},{80,64},{96,80},{112,96},{1... | collective-permute-start | bytes 589832 | tf_op jit(solution)/shard_map/ppermute | solution.py:189
  45.5 29.5 %copy-start.19 = (bf16[128,768]{1,0:T(8,128)(2,1)}, bf16[128,768]{1,0:T(8,128)(2,1)S(1)}, u32[]{:S(2)}) copy-start(bf16[128,768]{1,0:T(8,128)(2,1)S(1)} %collective-permute-done.refs_1_) | copy-start | bytes 589828
  45.5 6.1 %collective-permute-start.11 = (bf16[128,768]{1,0:T(8,128)(2,1)S(1)}, bf16[128,768]{1,0:T(8,128)(2,1)S(1)}, u32[]{:S(2)}, u32[]{:S(2)}) collective-permute-start(bf16[128,768]{1,0:T(8,128)(2,1)S(1)} %collective-permute-done.refs_1_), channel_id=1, source_target_pairs={{0,112},{16,0},{32,16},{48,32},{64,48},{80,64},{96,80},{112,96},{1... | collective-permute-start | bytes 589832 | tf_op jit(solution)/shard_map/ppermute | solution.py:189
  49.4 9.1 %collective-permute-start.8 = (bf16[128,768]{1,0:T(8,128)(2,1)S(1)}, bf16[128,768]{1,0:T(8,128)(2,1)S(1)}, u32[]{:S(2)}, u32[]{:S(2)}) collective-permute-start(bf16[128,768]{1,0:T(8,128)(2,1)S(1)} %collective-permute-done.refs_1_), channel_id=1, source_target_pairs={{0,16},{16,32},{32,48},{48,64},{64,80},{80,96},{96,112},{112,0},{1... | collective-permute-start | bytes 589832 | tf_op jit(solution)/shard_map/ppermute | solution.py:189
  49.5 25.5 %copy-start.21 = (bf16[128,768]{1,0:T(8,128)(2,1)}, bf16[128,768]{1,0:T(8,128)(2,1)S(1)}, u32[]{:S(2)}) copy-start(bf16[128,768]{1,0:T(8,128)(2,1)S(1)} %collective-permute-done.1.refs_2_) | copy-start | bytes 589828
  49.6 13.2 %collective-permute-start.2 = (bf16[128,768]{1,0:T(8,128)(2,1)S(1)}, bf16[128,768]{1,0:T(8,128)(2,1)S(1)}, u32[]{:S(2)}, u32[]{:S(2)}) collective-permute-start(bf16[128,768]{1,0:T(8,128)(2,1)S(1)} %collective-permute-done.1.refs_2_), channel_id=1, source_target_pairs={{0,16},{16,32},{32,48},{48,64},{64,80},{80,96},{96,112},{112,0},{1... | collective-permute-start | bytes 589832 | tf_op jit(solution)/shard_map/ppermute | solution.py:189
  51.7 11.1 %collective-permute-start.12 = (bf16[128,768]{1,0:T(8,128)(2,1)S(1)}, bf16[128,768]{1,0:T(8,128)(2,1)S(1)}, u32[]{:S(2)}, u32[]{:S(2)}) collective-permute-start(bf16[128,768]{1,0:T(8,128)(2,1)S(1)} %collective-permute-done.11.refs_12_), channel_id=1, source_target_pairs={{0,112},{16,0},{32,16},{48,32},{64,48},{80,64},{96,80},{112,96},{1... | collective-permute-start | bytes 589832 | tf_op jit(solution)/shard_map/ppermute | solution.py:189
  55.5 12.1 %collective-permute-start.6 = (bf16[128,768]{1,0:T(8,128)(2,1)S(1)}, bf16[128,768]{1,0:T(8,128)(2,1)S(1)}, u32[]{:S(2)}, u32[]{:S(2)}) collective-permute-start(bf16[128,768]{1,0:T(8,128)(2,1)S(1)} %collective-permute-done.5.refs_6_), channel_id=1, source_target_pairs={{0,112},{16,0},{32,16},{48,32},{64,48},{80,64},{96,80},{112,96},{1... | collective-permute-start | bytes 589832 | tf_op jit(solution)/shard_map/ppermute | solution.py:189
  58.6 9.0 %collective-permute-start.9 = (bf16[128,768]{1,0:T(8,128)(2,1)S(1)}, bf16[128,768]{1,0:T(8,128)(2,1)S(1)}, u32[]{:S(2)}, u32[]{:S(2)}) collective-permute-start(bf16[128,768]{1,0:T(8,128)(2,1)S(1)} %collective-permute-done.8.refs_9_), channel_id=1, source_target_pairs={{0,16},{16,32},{32,48},{48,64},{64,80},{80,96},{96,112},{112,0},{1... | collective-permute-start | bytes 589832 | tf_op jit(solution)/shard_map/ppermute | solution.py:189
  62.8 9.0 %collective-permute-start.3 = (bf16[128,768]{1,0:T(8,128)(2,1)S(1)}, bf16[128,768]{1,0:T(8,128)(2,1)S(1)}, u32[]{:S(2)}, u32[]{:S(2)}) collective-permute-start(bf16[128,768]{1,0:T(8,128)(2,1)S(1)} %collective-permute-done.2.refs_3_), channel_id=1, source_target_pairs={{0,16},{16,32},{32,48},{48,64},{64,80},{80,96},{96,112},{112,0},{1... | collective-permute-start | bytes 589832 | tf_op jit(solution)/shard_map/ppermute | solution.py:189
  62.8 9.0 %collective-permute-start.13 = (bf16[128,768]{1,0:T(8,128)(2,1)S(1)}, bf16[128,768]{1,0:T(8,128)(2,1)S(1)}, u32[]{:S(2)}, u32[]{:S(2)}) collective-permute-start(bf16[128,768]{1,0:T(8,128)(2,1)S(1)} %collective-permute-done.12.refs_13_), channel_id=1, source_target_pairs={{0,112},{16,0},{32,16},{48,32},{64,48},{80,64},{96,80},{112,96},{1... | collective-permute-start | bytes 589832 | tf_op jit(solution)/shard_map/ppermute | solution.py:189
  67.5 8.2 %collective-permute-start.7 = (bf16[128,768]{1,0:T(8,128)(2,1)S(1)}, bf16[128,768]{1,0:T(8,128)(2,1)S(1)}, u32[]{:S(2)}, u32[]{:S(2)}) collective-permute-start(bf16[128,768]{1,0:T(8,128)(2,1)S(1)} %collective-permute-done.6.refs_7_), channel_id=1, source_target_pairs={{0,112},{16,0},{32,16},{48,32},{64,48},{80,64},{96,80},{112,96},{1... | collective-permute-start | bytes 589832 | tf_op jit(solution)/shard_map/ppermute | solution.py:189
  67.6 8.2 %collective-permute-start.10 = (bf16[128,768]{1,0:T(8,128)(2,1)S(1)}, bf16[128,768]{1,0:T(8,128)(2,1)S(1)}, u32[]{:S(2)}, u32[]{:S(2)}) collective-permute-start(bf16[128,768]{1,0:T(8,128)(2,1)S(1)} %collective-permute-done.9.refs_10_), channel_id=1, source_target_pairs={{0,16},{16,32},{32,48},{48,64},{64,80},{80,96},{96,112},{112,0},{1... | collective-permute-start | bytes 589832 | tf_op jit(solution)/shard_map/ppermute | solution.py:189
  71.8 6.9 %collective-permute-start.4 = (bf16[128,768]{1,0:T(8,128)(2,1)S(1)}, bf16[128,768]{1,0:T(8,128)(2,1)S(1)}, u32[]{:S(2)}, u32[]{:S(2)}) collective-permute-start(bf16[128,768]{1,0:T(8,128)(2,1)S(1)} %collective-permute-done.3.refs_4_), channel_id=1, source_target_pairs={{0,16},{16,32},{32,48},{48,64},{64,80},{80,96},{96,112},{112,0},{1... | collective-permute-start | bytes 589832 | tf_op jit(solution)/shard_map/ppermute | solution.py:189
  71.8 6.9 %collective-permute-start.14 = (bf16[128,768]{1,0:T(8,128)(2,1)S(1)}, bf16[128,768]{1,0:T(8,128)(2,1)S(1)}, u32[]{:S(2)}, u32[]{:S(2)}) collective-permute-start(bf16[128,768]{1,0:T(8,128)(2,1)S(1)} %collective-permute-done.13.refs_14_), channel_id=1, source_target_pairs={{0,112},{16,0},{32,16},{48,32},{64,48},{80,64},{96,80},{112,96},{1... | collective-permute-start | bytes 589832 | tf_op jit(solution)/shard_map/ppermute | solution.py:189
  75.8 16.3 %copy-start.3 = (bf16[768,768]{1,0:T(8,128)(2,1)S(1)}, bf16[768,768]{1,0:T(8,128)(2,1)}, u32[]{:S(2)}) copy-start(bf16[768,768]{1,0:T(8,128)(2,1)} %w_ref.3) | copy-start | bytes 3538948
  (21 other events, 64.8 us)
Sparse Core Ops, SparseCore 0:
  14.3 42.6 all-gather.4
  58.8 39.9 all-gather.6

commit v2 on v0

v2 whole, which is shorter than its diff:
```python
import functools

import jax
import jax.numpy as jnp
from jax import lax
from jax.experimental import pallas as pl
from jax.experimental.pallas import tpu as pltpu
from jax.sharding import PartitionSpec as P

EPS = 1e-05
LOG2E = 1.4426950408889634
NEG = -1000000000.0 * LOG2E
F32 = jnp.float32
BF16 = jnp.bfloat16
MIB = 1024 * 1024


def dot(a, b, dims):
    return lax.dot_general(a, b, (dims, ((), ())), preferred_element_type=F32)


def params(mib):
    return pltpu.CompilerParams(vmem_limit_bytes=mib * MIB)


def norm_kernel(x_ref, gain_ref, out_ref):
    x = x_ref[...].astype(F32)
    center = jnp.mean(x, axis=-1, keepdims=True)
    d = x - center
    spread = jnp.mean(d * d, axis=-1, keepdims=True)
    out_ref[...] = (d * lax.rsqrt(spread + EPS) * gain_ref[...]).astype(BF16)


def norm_rows(x, gain):
    return pl.pallas_call(
        norm_kernel,
        out_shape=jax.ShapeDtypeStruct(x.shape, BF16),
        compiler_params=params(61),
    )(x, gain.reshape(1, -1))


def bias_kernel(step, pair_ref, gain_ref, proj_ref, out_ref, x_ref, sem, swap_ref):
    rows, nk, nc = pair_ref.shape
    heads = proj_ref.shape[0]
    parts = rows // step

    def fetch(i):
        return pltpu.make_async_copy(pair_ref.at[pl.ds(i * step, step)], x_ref.at[pl.ds(i * step, step)], sem.at[i])

    for i in range(parts):
        fetch(i).start()

    w = proj_ref[...] * gain_ref[...] * LOG2E
    w = w - jnp.mean(w, axis=-1, keepdims=True)
    hi = w.astype(BF16)
    rest = w - hi.astype(F32)
    mid = rest.astype(BF16)
    low = (rest - mid.astype(F32)).astype(BF16)
    none = jnp.zeros((heads, nc), BF16)
    mean = jnp.full((heads, nc), 1.0 / nc, BF16)
    w = jnp.concatenate(
        [jnp.concatenate([hi, mid, low, none], axis=0), jnp.concatenate([none, none, none, mean], axis=0)], axis=1
    )
    row = lax.broadcasted_iota(jnp.int32, (nc, nc), 0)
    col = lax.broadcasted_iota(jnp.int32, (nc, nc), 1)
    center = (jnp.where(row == col, 1.0, 0.0) - 1.0 / nc).astype(BF16)

    for i in range(parts):
        fetch(i).wait()
        x = x_ref[i * step : (i + 1) * step].reshape(step * nk, nc)
        d = dot(x, center, ((1,), (0,)))
        r = dot(w, jnp.concatenate([x, (d * d).astype(BF16)], axis=1), ((1,), (1,)))
        spread = r[3 * heads : 3 * heads + 1]
        r = (r[:heads] + r[heads : 2 * heads] + r[2 * heads : 3 * heads]) * lax.rsqrt(spread + EPS)
        for q in range(step):
            swap_ref[pl.ds(i * step + q, heads, stride=rows), :] = r[:, q * nk : (q + 1) * nk]

    for h in range(heads):
        out_ref[:, h * rows : (h + 1) * rows] = swap_ref[h * rows : (h + 1) * rows, :].astype(BF16).T


def pair_bias(pair, gain, proj_t):
    rows, nk, nc = pair.shape
    heads = proj_t.shape[0]
    step = 16
    vmem = pl.BlockSpec(memory_space=pltpu.VMEM)
    return pl.pallas_call(
        functools.partial(bias_kernel, step),
        in_specs=[pl.BlockSpec(memory_space=pl.ANY), vmem, vmem],
        out_specs=vmem,
        out_shape=jax.ShapeDtypeStruct((nk, heads * rows), BF16),
        scratch_shapes=[
            pltpu.VMEM((rows, nk, nc), BF16),
            pltpu.SemaphoreType.DMA((rows // step,)),
            pltpu.VMEM((heads * rows, nk), F32),
        ],
        compiler_params=params(61),
        cost_estimate=pl.CostEstimate(
            flops=rows * nk * nc * 400, bytes_accessed=rows * nk * nc * 2, transcendentals=0
        ),
    )(pair, gain.reshape(1, -1), proj_t)


def whole(*s):
    return pl.BlockSpec(s, lambda i: (0,) * len(s))


def prepare_kernel(
    x_ref, wq_ref, wk_ref, wv_ref, wg_ref, chain_row_ref, chain_ref, mask_ref, gain_ref,
    q_ref, gate_ref, wide_ref, turned_ref, hot_ref, limit_ref,
):
    pairs, depth, lanes = q_ref.shape
    n = lanes // 2
    width = x_ref.shape[1]
    hdim = width // (2 * pairs)
    x = x_ref[...]
    q = (dot(wq_ref[...].T, x, ((1,), (1,))) * (hdim**-0.5 * LOG2E)).astype(BF16)
    gate_ref[...] = jax.nn.sigmoid(dot(wg_ref[...].T, x, ((1,), (1,))).astype(BF16).astype(F32))
    kinds = lax.broadcasted_iota(jnp.int32, (8, n), 0)
    same = kinds == chain_row_ref[...]
    none = jnp.zeros((hdim, n), BF16)
    for i in range(pairs):
        for j in range(2):
            h = 2 * i + j
            own = q[h * hdim : (h + 1) * hdim]
            gain = jnp.where(same, gain_ref[h] * LOG2E, 0.0)
            hi = gain.astype(BF16)
            rest = gain - hi.astype(F32)
            mid = rest.astype(BF16)
            low = (rest - mid.astype(F32)).astype(BF16)
            last = jnp.concatenate([hi, mid, low, jnp.zeros((depth - 2 * hdim - 24, n), BF16)], axis=0)
            q_ref[i, :, j * n : (j + 1) * n] = jnp.concatenate([none, own, last] if j else [own, none, last], axis=0)
    wide_ref[...] = jnp.zeros_like(wide_ref)
    for i in range(pairs):
        wide_ref[:, i * depth : i * depth + 2 * hdim] = wk_ref[:, 2 * i * hdim : (2 * i + 2) * hdim]
    turned_ref[...] = wv_ref[...].T
    step = 256
    lane = lax.broadcasted_iota(jnp.int32, (step, depth), 1) - 2 * hdim
    kind = jnp.where((lane >= 0) & (lane < 24), lane % 8, -1)
    for c in range(0, chain_ref.shape[0], step):
        hot_ref[c : c + step, :] = (chain_ref[c : c + step, :] == kind).astype(F32).astype(BF16)
        keep = jnp.broadcast_to(mask_ref[c : c + step, :], (step, limit_ref.shape[1]))
        limit_ref[c : c + step, :] = jnp.where(keep > 0, F32(3.0e38), F32(NEG))


def prepare(x, w, chain_index, chain_query, key_mask, chain_gain):
    n, width = x.shape
    heads = chain_gain.shape[0]
    keys = chain_index.shape[0]
    pairs, depth = heads // 2, 128
    shapes = [
        ((pairs, depth, 2 * n), BF16),
        ((width, n), F32),
        ((width, pairs * depth), BF16),
        ((width, width), BF16),
        ((keys, depth), BF16),
        ((keys, n), F32),
    ]
    return pl.pallas_call(
        prepare_kernel,
        grid=(1,),
        in_specs=[whole(n, width)]
        + [pl.BlockSpec((width, width), lambda i, j=j: (0, j)) for j in range(4)]
        + [whole(1, n), whole(keys, 1), whole(keys, 1), pl.BlockSpec(memory_space=pltpu.SMEM)],
        out_specs=[whole(*d) for d, _ in shapes],
        out_shape=[jax.ShapeDtypeStruct(d, t) for d, t in shapes],
        compiler_params=params(61),
        cost_estimate=pl.CostEstimate(flops=8 * n * width * width, bytes_accessed=12 * MIB, transcendentals=0),
    )(x, w, w, w, w, chain_query.reshape(1, n), chain_index.reshape(keys, 1), key_mask.reshape(keys, 1), chain_gain)


def kv_kernel(n, pos_ref, wide_ref, turned_ref, hot_ref, *refs):
    blocks, (k_ref, v_ref) = refs[:-2], refs[-2:]
    depth = hot_ref.shape[1]
    pairs = wide_ref.shape[1] // depth
    x = jnp.concatenate([b[...] for b in blocks], axis=0)
    for i in range(0, x.shape[0] // n, 2):
        rows = slice(i * n, (i + 2) * n)
        hot = jnp.concatenate(
            [hot_ref[pl.ds(pl.multiple_of(pos_ref[i + j] * n, n), n), :] for j in range(2)], axis=0
        )
        y = dot(x[rows], wide_ref[...], ((1,), (0,))).astype(BF16)
        k_ref[rows, :] = y + jnp.concatenate([hot] * pairs, axis=1)
        v_ref[:, rows] = dot(turned_ref[...], x[rows], ((1,), (1,))).astype(BF16)


def keys_values(pos, wide, turned, hot, blocks):
    tokens = sum(b.shape[0] for b in blocks)
    lanes, width = wide.shape[1], turned.shape[0]
    vmem = pl.BlockSpec(memory_space=pltpu.VMEM)
    return pl.pallas_call(
        functools.partial(kv_kernel, tokens // pos.shape[0]),
        in_specs=[pl.BlockSpec(memory_space=pltpu.SMEM)] + [vmem] * (3 + len(blocks)),
        out_specs=[vmem, vmem],
        out_shape=[
            jax.ShapeDtypeStruct((tokens, lanes), BF16),
            jax.ShapeDtypeStruct((width, tokens), BF16),
        ],
        compiler_params=params(61),
        cost_estimate=pl.CostEstimate(flops=5 * width * width * tokens, bytes_accessed=8 * MIB, transcendentals=0),
    )(pos, wide, turned, hot, *blocks)


def attend_kernel(n, batches, pos_ref, q_hbm, bias_ref, limit_hbm, gate_hbm, w_hbm, *refs):
    k_hbm, v_hbm = refs[:batches], refs[batches : 2 * batches]
    out_ref, q_ref, limit_ref, gate_ref, w_ref, k_ref, v_ref, b_ref, sem, hid_ref, s_ref, p_ref = refs[2 * batches :]
    pairs, depth, lanes = q_ref.shape
    nq = lanes // 2
    tokens = limit_ref.shape[0]
    hdim = w_ref.shape[0] // (2 * pairs)
    groups = b_ref.shape[0]
    per = pairs // groups
    starts = [0]
    for k in k_hbm:
        starts.append(starts[-1] + k.shape[0])

    def fetch(src, dst, i):
        return pltpu.make_async_copy(src, dst, sem.at[i])

    def fetch_keys(g):
        cols = slice(g * per * depth, (g + 1) * per * depth)
        return [
            fetch(k.at[:, cols], k_ref.at[starts[b] : starts[b + 1], cols], 4 + b * groups + g)
            for b, k in enumerate(k_hbm)
        ]

    def fetch_values(g):
        rows = slice(2 * g * per * hdim, 2 * (g + 1) * per * hdim)
        return [
            fetch(v.at[rows, :], v_ref.at[rows, starts[b] : starts[b + 1]], 4 + (batches + b) * groups + g)
            for b, v in enumerate(v_hbm)
        ]

    def bias_sem(g):
        return 4 + 2 * batches * groups + g

    fetch(q_hbm, q_ref, 0).start()
    fetch(limit_hbm, limit_ref, 1).start()
    for g in range(groups):
        for copy in fetch_keys(g):
            copy.start()
        cols = slice(g * per * lanes, (g + 1) * per * lanes)
        for c in range(tokens // n):
            at = pl.multiple_of(pos_ref[c] * n, n)
            fetch(bias_ref.at[pl.ds(at, n), cols], b_ref.at[g, pl.ds(c * n, n)], bias_sem(g)).start()
        for copy in fetch_values(g):
            copy.start()
        if g == 0:
            fetch(gate_hbm, gate_ref, 2).start()
    fetch(w_hbm, w_ref, 3).start()
    fetch(q_hbm, q_ref, 0).wait()
    fetch(limit_hbm, limit_ref, 1).wait()

    def scores(i):
        g, c0 = i // per, i % per * lanes
        if i % per == 0:
            for copy in fetch_keys(g):
                copy.wait()
            fetch(bias_ref.at[:, g * per * lanes : (g + 1) * per * lanes], b_ref.at[g], bias_sem(g)).wait()
        top = None
        for c in range(tokens // n):
            s = dot(k_ref[c * n : (c + 1) * n, i * depth : (i + 1) * depth], q_ref[i], ((1,), (0,)))
            mask = limit_ref[pl.ds(pl.multiple_of(pos_ref[c] * n, n), n), :]
            s = s + b_ref[g, c * n : (c + 1) * n, c0 : c0 + lanes].astype(F32)
            s = jnp.minimum(s, jnp.concatenate([mask, mask], axis=1))
            s_ref[i % 2, c * n : (c + 1) * n, :] = s
            t = jnp.max(s.reshape(n // 8, 8, lanes), axis=0)
            top = t if top is None else jnp.maximum(top, t)
        return jnp.max(top, axis=0, keepdims=True)

    def soften(i, top):
        total = None
        for c in range(tokens // n):
            p = jnp.exp2(s_ref[i % 2, c * n : (c + 1) * n, :] - top)
            p_ref[i % 2, c * n : (c + 1) * n, :] = p.astype(BF16)
            t = jnp.sum(p.reshape(n // 8, 8, lanes), axis=0)
            total = t if total is None else total + t
        return jnp.sum(total, axis=0, keepdims=True)

    def weigh(i, total):
        rows = slice(2 * i * hdim, (2 * i + 2) * hdim)
        if i == 0:
            fetch(gate_hbm, gate_ref, 2).wait()
        if i % per == 0:
            for copy in fetch_values(i // per):
                copy.wait()
        o = dot(v_ref[rows, :], p_ref[i % 2], ((1,), (0,))) / total
        o = jnp.concatenate([o[:hdim, :nq], o[hdim:, nq:]], axis=0)
        hid_ref[rows, :] = (gate_ref[rows, :] * o).astype(BF16)

    top = scores(0)
    for i in range(pairs):
        total = soften(i, top)
        if i + 1 < pairs:
            top = scores(i + 1)
        weigh(i, total)

    fetch(w_hbm, w_ref, 3).wait()
    out_ref[...] = dot(hid_ref[...], w_ref[...], ((0,), (0,))).astype(BF16)


def attend(pos, q, ks, vs, bias, limit, gates_t, w_out):
    pairs, _, lanes = q.shape
    width = w_out.shape[0]
    tokens = bias.shape[0]
    nq = lanes // 2
    groups = 4
    return pl.pallas_call(
        functools.partial(attend_kernel, tokens // pos.shape[0], len(ks)),
        in_specs=[pl.BlockSpec(memory_space=pltpu.SMEM)] + [pl.BlockSpec(memory_space=pl.ANY)] * (5 + 2 * len(ks)),
        out_specs=pl.BlockSpec(memory_space=pltpu.VMEM),
        out_shape=jax.ShapeDtypeStruct((nq, width), BF16),
        scratch_shapes=[
            pltpu.VMEM(q.shape, BF16),
            pltpu.VMEM(limit.shape, F32),
            pltpu.VMEM(gates_t.shape, F32),
            pltpu.VMEM(w_out.shape, BF16),
            pltpu.VMEM((tokens, ks[0].shape[1]), BF16),
            pltpu.VMEM((width, tokens), BF16),
            pltpu.VMEM((groups, tokens, pairs // groups * lanes), BF16),
            pltpu.SemaphoreType.DMA((4 + (2 * len(ks) + 1) * groups,)),
            pltpu.VMEM((width, nq), BF16),
            pltpu.VMEM((2, tokens, lanes), F32),
            pltpu.VMEM((2, tokens, lanes), BF16),
        ],
        compiler_params=params(61),
        cost_estimate=pl.CostEstimate(
            flops=pairs * lanes * tokens * 1024, bytes_accessed=8 * MIB, transcendentals=pairs * lanes * tokens
        ),
    )(pos, q, bias, limit, gates_t, w_out, *ks, *vs)


def shift_z(x, by):
    def to(i):
        return (i // 8) * 8 + (i % 8 + by) % 8

    return lax.ppermute(x, "pb", [(i, to(i)) for i in range(16)])


def swap_y(x):
    return lax.ppermute(x, "pb", [(i, (i + 8) % 16) for i in range(16)])


def attended_rows(own, prepared, bias, w_out):
    me = lax.axis_index("pb")
    y, z = me // 8, me % 8
    n = own.shape[0]
    both = jnp.concatenate([own, swap_y(own)], axis=0)

    def places(by):
        return [y * 8 + (z + by) % 8, (1 - y) * 8 + (z + by) % 8]

    ks, vs, pos = [], [], []

    def project(arrays, at):
        at = jnp.stack(at).astype(jnp.int32)
        k, v = keys_values(at, wide, turned, hot, arrays)
        ks.append(k)
        vs.append(v)
        pos.append(at)

    right, left = shift_z(both, 1), shift_z(both, -1)
    right, left, prepared = lax.optimization_barrier((right, left, prepared))
    q, gates_t, wide, turned, hot, limit = prepared
    waiting, at = [both, right, left], places(0) + places(-1) + places(1)
    for hop in range(2, 4):
        next_right, next_left = shift_z(right, 1), shift_z(left, -1)
        project(waiting, at)
        right, left, ks[-1], vs[-1] = lax.optimization_barrier((next_right, next_left, ks[-1], vs[-1]))
        waiting, at = [right, left], places(-hop) + places(hop)
    last = [shift_z(right[:n], 1), shift_z(left[n:], -1)]
    project(waiting, at)
    project(last, places(4))
    return attend(jnp.concatenate(pos), q, ks, vs, bias, limit, gates_t, w_out)


def body(tokens, pair, token_chain_index, key_mask, norm_gain, pair_gain, pair_proj, chain_gain, w_qkvg, w_out):
    nq = tokens.shape[1]

    normed = norm_rows(tokens[0], norm_gain)
    tile, normed = lax.optimization_barrier((pair, normed))
    bias = pair_bias(tile, pair_gain, pair_proj.T)
    bias_all = lax.all_gather(bias, "ka", axis=0, tiled=True)
    chain_query = lax.dynamic_slice_in_dim(token_chain_index, lax.axis_index("pb") * nq, nq)
    prepared = prepare(normed, w_qkvg, token_chain_index, chain_query, key_mask, chain_gain)
    return attended_rows(normed, prepared, bias_all, w_out)[None]


def solution(mesh):
    in_specs = (P("ka", "pb", None), P("pb", "ka", None), P(), P(), P(), P(), P(), P(), P(), P())
    out_specs = P("ka", "pb", None)
    return jax.shard_map(body, mesh=mesh, in_specs=in_specs, out_specs=out_specs, check_vma=False)
```

time: 252 us -> 96.9 us (0.38)
  waiting for transfers between devices: 163 us -> 6.36 us
  Pallas kernels: 0 us -> 48.1 us
  matrix products: 47.3 us -> 0 us
  other arithmetic: 22 us -> 1.84 us
  starting transfers between devices: 0.04 us -> 19.5 us
  local copies, waits for them, and re-layouts: 4.38 us -> 7.29 us
    all_gather x2 -> x1, waiting for transfers between devices: 163 us -> 0.01 us  [body(): bias_all = lax.all_gather(bias, 'ka', axis=0, tiled=True)]
    pallas_call x0 -> x8, Pallas kernels: none -> 48.1 us  [the longest x4 19.5 us: keys_values(): pl.pallas_call(functools.partial(kv_kernel, tokens // pos.shape[0]), in_s...]
    dot_general x6 -> x0, matrix products: 47.3 us -> none  [the longest x1 15.5 us: apply_attention(): jnp.einsum('qhd,khd->hqk', query_heads, key_heads, preferred_element_type...]
    ppermute x0 -> x9, starting transfers between devices: none -> 19.5 us  [the longest x8 16.2 us: shift_z(): return lax.ppermute(x, 'pb', [(i, to(i)) for i in range(16)])]
    reduce_sum x5 -> x0, other arithmetic: 18.8 us -> none  [the longest x1 8.14 us: apply_attention(): total = jnp.sum(expo, axis=-1)]
    ppermute x0 -> x9, waiting for transfers between devices: none -> 6.34 us  [the longest x1 4.93 us: swap_y(): return lax.ppermute(x, 'pb', [(i, (i + 8) % 16) for i in range(16)])]
    reshape x0 -> x4, local copies, waits for them, and re-layouts: none -> 4.58 us  [the longest x1 1.37 us: prepare(): chain_index.reshape(keys, 1)]
    slice x1 -> x2, local copies, waits for them, and re-layouts: 3.24 us -> 0.03 us  [attended_rows(): last = [shift_z(right[:n], 1), shift_z(left[n:], -1)]]
  transfers between devices with their start and end apart: 2 -> 10, of which waited for: 2 -> 3; matrix products, arithmetic and copies ran while one was open for 13% -> 7% of each run, Pallas kernels for 0% -> 27%
where the time goes in v2:
time: 96.9 us; the launch traced here: 96.7 us
  Pallas kernels  48.1 us (50%)
  starting transfers between devices  19.5 us (20%)
  between operations  13.5 us (14%)
  local copies, waits for them, and re-layouts  7.29 us (8%)
  waiting for transfers between devices  6.36 us (7%)
  other arithmetic  1.84 us (2%)
    pallas_call x4, Pallas kernels, keys_values(): pl.pallas_call(functools.partial(kv_kernel, tokens // pos.shape[0]), in_s...  19.5 us
    ppermute x8, starting transfers between devices, shift_z(): return lax.ppermute(x, 'pb', [(i, to(i)) for i in range(16)])  16.2 us
    pallas_call x1, Pallas kernels, attend(): pl.pallas_call(functools.partial(attend_kernel, tokens // pos.shape[0], l...  11.7 us
    pallas_call x1, Pallas kernels, pair_bias(): pl.pallas_call(functools.partial(bias_kernel, step), in_specs=[pl.BlockSp...  8.11 us
    pallas_call x1, Pallas kernels, prepare(): pl.pallas_call(prepare_kernel, grid=(1,), in_specs=[whole(n, width)] + [p...  7.02 us
    ppermute x1, waiting for transfers between devices, swap_y(): return lax.ppermute(x, 'pb', [(i, (i + 8) % 16) for i in range(16)])  4.93 us
    ppermute x1, starting transfers between devices, swap_y(): return lax.ppermute(x, 'pb', [(i, (i + 8) % 16) for i in range(16)])  3.28 us
  transfers between devices with their start and end apart: 10, of which 3 were waited for; matrix products, arithmetic and copies ran while one was open for 7% of the time, Pallas kernels for 27%

profile of v2, /device:TPU:2, one launch (start us, length us, event | category | flops | bytes accessed | tf_op | source)
XLA Modules:
  0.0 96.7 jit_solution(12477535727113808292)
XLA Ops:
  6.5 1.3 %reshape.15.gain_ref = f32[1,768]{1,0:T(1,128)} reshape(f32[768]{0:T(1024)} %param.14) | data formatting | bytes 6144 | tf_op jit(solution)/shard_map/reshape | solution.py:39
  7.8 1.8 %shard_map.100.x_ref = bf16[128,768]{1,0:T(8,128)(2,1)} custom-call(bf16[128,768]{1,0:T(8,128)(2,1)} %bitcast.24, f32[1,768]{1,0:T(1,128)} %reshape.15.gain_ref), custom_call_target="tpu_custom_call" | custom-call | tf_op jit(solution)/shard_map/pallas_call | solution.py:35
  9.7 8.1 %shard_map.102 = bf16[128,2048]{1,0:T(8,128)(2,1)} custom-call(bf16[128,128,128]{2,1,0:T(8,128)(2,1)} %pair_ref, f32[1,128]{1,0:T(1,128)} %bitcast.28, f32[16,128]{1,0:T(8,128)} %bitcast.25), custom_call_target="tpu_custom_call" | custom-call | flops 838860800 | bytes 4194304 | tf_op jit(solution)/shard_map/pallas_call | solution.py:87
  17.8 3.3 %collective-permute-start = (bf16[128,768]{1,0:T(8,128)(2,1)S(1)}, bf16[128,768]{1,0:T(8,128)(2,1)S(1)}, u32[]{:S(2)}, u32[]{:S(2)}) collective-permute-start(bf16[128,768]{1,0:T(8,128)(2,1)S(1)} %copy-done), channel_id=1, source_target_pairs={{0,128},{16,144},{32,160},{48,176},{64,192},{80,208},{96,224},{112... | collective-permute-start | bytes 589832 | tf_op jit(solution)/shard_map/ppermute | solution.py:341
  21.1 4.9 %collective-permute-done = bf16[128,768]{1,0:T(8,128)(2,1)S(1)} collective-permute-done((bf16[128,768]{1,0:T(8,128)(2,1)S(1)}, bf16[128,768]{1,0:T(8,128)(2,1)S(1)}, u32[]{:S(2)}, u32[]{:S(2)}) %collective-permute-start) | collective-permute-done | bytes 196640 | tf_op jit(solution)/shard_map/ppermute | solution.py:341
  26.1 2.0 %collective-permute-start.1 = (bf16[256,768]{1,0:T(8,128)(2,1)S(1)}, bf16[256,768]{1,0:T(8,128)(2,1)S(1)}, u32[]{:S(2)}, u32[]{:S(2)}) collective-permute-start(bf16[256,768]{1,0:T(8,128)(2,1)S(1)} %constant_dynamic-update-slice_fusion.refs_0_), channel_id=1, source_target_pairs={{0,16},{16,32},{32,48},{48,64},{64,80},{80,96},{96,112},{112,0},{1... | collective-permute-start | bytes 1179656 | tf_op jit(solution)/shard_map/ppermute | solution.py:337
  28.1 4.0 %collective-permute-start.2 = (bf16[256,768]{1,0:T(8,128)(2,1)S(1)}, bf16[256,768]{1,0:T(8,128)(2,1)S(1)}, u32[]{:S(2)}, u32[]{:S(2)}) collective-permute-start(bf16[256,768]{1,0:T(8,128)(2,1)S(1)} %constant_dynamic-update-slice_fusion.refs_0_), channel_id=1, source_target_pairs={{0,112},{16,0},{32,16},{48,32},{64,48},{80,64},{96,80},{112,96},{1... | collective-permute-start | bytes 1179656 | tf_op jit(solution)/shard_map/ppermute | solution.py:337
  32.1 1.4 %copy.11.chain_ref = s32[2048,1]{1,0:T(8,128)} copy(s32[2048,1]{0,1:T(1,128)S(1)} %bitcast.27) | data formatting | bytes 16384 | tf_op jit(solution)/shard_map/reshape | solution.py:169
  33.5 1.3 %copy.12.mask_ref = s32[2048,1]{1,0:T(8,128)} copy(s32[2048,1]{0,1:T(1,128)S(1)} %bitcast.26) | data formatting | bytes 16384 | tf_op jit(solution)/shard_map/reshape | solution.py:169
  35.4 7.0 %shard_map.101 = (bf16[8,128,256]{2,1,0:T(8,128)(2,1)}, f32[768,128]{1,0:T(8,128)}, bf16[768,1024]{1,0:T(8,128)(2,1)}, bf16[768,768]{1,0:T(8,128)(2,1)}, bf16[2048,128]{1,0:T(8,128)(2,1)}, /*index=5*/f32[2048,128]{1,0:T(8,128)}) custom-call(bf16[128,768]{1,0:T(8,128)(2,1)} %shard_map.100.x_ref, bf16[768,3072]{1,0:T(8,128)(2,1)} %wg_ref.1, ...), custom_call_target="tpu_custom_call" | custom-call | flops 603979776 | bytes 12582912 | tf_op jit(solution)/shard_map/pallas_call | solution.py:159
  42.6 3.2 %collective-permute-start.4 = (bf16[256,768]{1,0:T(8,128)(2,1)S(1)}, bf16[256,768]{1,0:T(8,128)(2,1)S(1)}, u32[]{:S(2)}, u32[]{:S(2)}) collective-permute-start(bf16[256,768]{1,0:T(8,128)(2,1)S(1)} %collective-permute-done.2.refs_2_), channel_id=1, source_target_pairs={{0,112},{16,0},{32,16},{48,32},{64,48},{80,64},{96,80},{112,96},{1... | collective-permute-start | bytes 1179656 | tf_op jit(solution)/shard_map/ppermute | solution.py:337
  45.8 0.7 stack.76.pos_ref
  46.4 6.2 %shard_map.103 = (bf16[768,1024]{1,0:T(8,128)(2,1)}, bf16[768,768]{1,0:T(8,128)(2,1)}) custom-call(s32[6]{0:T(128)} %stack.76.pos_ref, bf16[768,1024]{1,0:T(8,128)(2,1)} %get-tuple-element.50.wide_ref, bf16[768,768]{1,0:T(8,128)(2,1)} %get-tuple-element.51.turned_ref, bf16[2048,128]{1,0:T(8,128)(2,1)} %get-tuple-element.52.hot_ref, ...), custom_call_target="tpu_custom_call" | custom-call | flops 2264924160 | bytes 8388608 | tf_op jit(solution)/shard_map/pallas_call | solution.py:191
  52.6 0.8 collective-permute-done.3.refs_0_
  53.5 3.2 %collective-permute-start.6 = (bf16[256,768]{1,0:T(8,128)(2,1)S(1)}, bf16[256,768]{1,0:T(8,128)(2,1)S(1)}, u32[]{:S(2)}, u32[]{:S(2)}) collective-permute-start(bf16[256,768]{1,0:T(8,128)(2,1)S(1)} %collective-permute-done.4.refs_1_), channel_id=1, source_target_pairs={{0,112},{16,0},{32,16},{48,32},{64,48},{80,64},{96,80},{112,96},{1... | collective-permute-start | bytes 1179656 | tf_op jit(solution)/shard_map/ppermute | solution.py:337
  56.7 0.7 pad_add_fusion.2.pos_ref
  58.0 4.8 %shard_map.104 = (bf16[512,1024]{1,0:T(8,128)(2,1)}, bf16[768,512]{1,0:T(8,128)(2,1)}) custom-call(s32[4]{0:T(128)} %pad_add_fusion.pos_ref, bf16[768,1024]{1,0:T(8,128)(2,1)} %get-tuple-element.50.wide_ref, bf16[768,768]{1,0:T(8,128)(2,1)} %get-tuple-element.51.turned_ref, bf16[2048,128]{1,0:T(8,128)(2,1)} %get-tuple-element.52.hot_ref, ...), custom_call_target="tpu_custom_call" | custom-call | flops 1509949440 | bytes 8388608 | tf_op jit(solution)/shard_map/pallas_call | solution.py:191
  63.4 1.9 %collective-permute-start.7 = (bf16[128,768]{1,0:T(8,128)(2,1)S(1)}, bf16[128,768]{1,0:T(8,128)(2,1)S(1)}, u32[]{:S(2)}, u32[]{:S(2)}) collective-permute-start(bf16[128,768]{1,0:T(8,128)(2,1)S(1)} %slice.6), channel_id=1, source_target_pairs={{0,16},{16,32},{32,48},{48,64},{64,80},{80,96},{96,112},{112,0},{1... | collective-permute-start | bytes 589832 | tf_op jit(solution)/shard_map/ppermute | solution.py:337
  65.4 1.7 %collective-permute-start.8 = (bf16[128,768]{1,0:T(8,128)(2,1)S(1)}, bf16[128,768]{1,0:T(8,128)(2,1)S(1)}, u32[]{:S(2)}, u32[]{:S(2)}) collective-permute-start(bf16[128,768]{1,0:T(8,128)(2,1)S(1)} %slice.7), channel_id=1, source_target_pairs={{0,112},{16,0},{32,16},{48,32},{64,48},{80,64},{96,80},{112,96},{1... | collective-permute-start | bytes 589832 | tf_op jit(solution)/shard_map/ppermute | solution.py:337
  68.3 4.8 %shard_map.105 = (bf16[512,1024]{1,0:T(8,128)(2,1)}, bf16[768,512]{1,0:T(8,128)(2,1)}) custom-call(s32[4]{0:T(128)} %pad_add_fusion.1.pos_ref, bf16[768,1024]{1,0:T(8,128)(2,1)} %get-tuple-element.50.wide_ref, bf16[768,768]{1,0:T(8,128)(2,1)} %get-tuple-element.51.turned_ref, bf16[2048,128]{1,0:T(8,128)(2,1)} %get-tuple-element.52.hot_ref, ...), custom_call_target="tpu_custom_call" | custom-call | flops 1509949440 | bytes 8388608 | tf_op jit(solution)/shard_map/pallas_call | solution.py:191
  73.1 0.7 copy-done.1
  73.8 0.7 copy-done.2
  74.5 3.6 %shard_map.106 = (bf16[256,1024]{1,0:T(8,128)(2,1)}, bf16[768,256]{1,0:T(8,128)(2,1)}) custom-call(s32[2]{0:T(128)} %pad_add_fusion.2.pos_ref, bf16[768,1024]{1,0:T(8,128)(2,1)} %get-tuple-element.50.wide_ref, bf16[768,768]{1,0:T(8,128)(2,1)} %get-tuple-element.51.turned_ref, bf16[2048,128]{1,0:T(8,128)(2,1)} %get-tuple-element.52.hot_ref, ...), custom_call_target="tpu_custom_call" | custom-call | flops 754974720 | bytes 8388608 | tf_op jit(solution)/shard_map/pallas_call | solution.py:191
  78.1 11.7 %shard_map.107 = bf16[128,768]{1,0:T(8,128)(2,1)} custom-call(s32[16]{0:T(128)} %concatenate.7.pos_ref, bf16[8,128,256]{2,1,0:T(8,128)(2,1)} %get-tuple-element.44.q_hbm, bf16[2048,2048]{1,0:T(8,128)(2,1)} %all-gather.2.cloned.1.call-done.bias_ref, f32[2048,128]{1,0:T(8,128)} %get-tuple-element.46.limit_hbm, f32[768,128]{1,0:T(8,128)} %get-tuple-element.47.gate_hbm, ...), custom_call_target="tpu_custom_call" | custom-call | flops 4294967296 | bytes 8388608 | tf_op jit(solution)/shard_map/pallas_call | solution.py:308
  (42 shorter events, 3.3 us)
Async XLA Ops:
  6.5 71.6 %all-gather.2.cloned.1.call-start = ((), (), s32[]{:S(2)}) async-start(), calls=%async_computation | async-start | bytes 8912896 | tf_op jit(solution)/shard_map/all_gather | solution.py:383
  9.7 8.2 %copy-start = (bf16[128,768]{1,0:T(8,128)(2,1)S(1)}, bf16[128,768]{1,0:T(8,128)(2,1)}, u32[]{:S(2)}) copy-start(bf16[128,768]{1,0:T(8,128)(2,1)} %shard_map.100.x_ref) | copy-start | bytes 589828
  9.7 22.5 %copy-start.7 = (s32[2048]{0:T(1024)S(1)}, s32[2048]{0:T(1024)}, u32[]{:S(2)}) copy-start(s32[2048]{0:T(1024)} %param.12) | copy-start | bytes 24580
  17.8 15.7 %copy-start.6 = (s32[2048]{0:T(1024)S(1)}, s32[2048]{0:T(1024)}, u32[]{:S(2)}) copy-start(s32[2048]{0:T(1024)} %param.13) | copy-start | bytes 24580
  17.8 8.2 %collective-permute-start = (bf16[128,768]{1,0:T(8,128)(2,1)S(1)}, bf16[128,768]{1,0:T(8,128)(2,1)S(1)}, u32[]{:S(2)}, u32[]{:S(2)}) collective-permute-start(bf16[128,768]{1,0:T(8,128)(2,1)S(1)} %copy-done), channel_id=1, source_target_pairs={{0,128},{16,144},{32,160},{48,176},{64,192},{80,208},{96,224},{112... | collective-permute-start | bytes 589832 | tf_op jit(solution)/shard_map/ppermute | solution.py:341
  26.1 16.4 %copy-start.5 = (bf16[256,768]{1,0:T(8,128)(2,1)}, bf16[256,768]{1,0:T(8,128)(2,1)S(1)}, u32[]{:S(2)}) copy-start(bf16[256,768]{1,0:T(8,128)(2,1)S(1)} %constant_dynamic-update-slice_fusion.refs_0_) | copy-start | bytes 1179652
  26.1 16.4 %collective-permute-start.1 = (bf16[256,768]{1,0:T(8,128)(2,1)S(1)}, bf16[256,768]{1,0:T(8,128)(2,1)S(1)}, u32[]{:S(2)}, u32[]{:S(2)}) collective-permute-start(bf16[256,768]{1,0:T(8,128)(2,1)S(1)} %constant_dynamic-update-slice_fusion.refs_0_), channel_id=1, source_target_pairs={{0,16},{16,32},{32,48},{48,64},{64,80},{80,96},{96,112},{112,0},{1... | collective-permute-start | bytes 1179656 | tf_op jit(solution)/shard_map/ppermute | solution.py:337
  28.1 14.4 %collective-permute-start.2 = (bf16[256,768]{1,0:T(8,128)(2,1)S(1)}, bf16[256,768]{1,0:T(8,128)(2,1)S(1)}, u32[]{:S(2)}, u32[]{:S(2)}) collective-permute-start(bf16[256,768]{1,0:T(8,128)(2,1)S(1)} %constant_dynamic-update-slice_fusion.refs_0_), channel_id=1, source_target_pairs={{0,112},{16,0},{32,16},{48,32},{64,48},{80,64},{96,80},{112,96},{1... | collective-permute-start | bytes 1179656 | tf_op jit(solution)/shard_map/ppermute | solution.py:337
  42.4 4.0 %copy-start.10 = (bf16[256,768]{1,0:T(8,128)(2,1)}, bf16[256,768]{1,0:T(8,128)(2,1)S(1)}, u32[]{:S(2)}) copy-start(bf16[256,768]{1,0:T(8,128)(2,1)S(1)} %collective-permute-done.1.refs_1_) | copy-start | bytes 1179652
  42.5 4.0 %copy-start.11 = (bf16[256,768]{1,0:T(8,128)(2,1)}, bf16[256,768]{1,0:T(8,128)(2,1)S(1)}, u32[]{:S(2)}) copy-start(bf16[256,768]{1,0:T(8,128)(2,1)S(1)} %collective-permute-done.2.refs_2_) | copy-start | bytes 1179652
  42.5 10.9 %collective-permute-start.3 = (bf16[256,768]{1,0:T(8,128)(2,1)S(1)}, bf16[256,768]{1,0:T(8,128)(2,1)S(1)}, u32[]{:S(2)}, u32[]{:S(2)}) collective-permute-start(bf16[256,768]{1,0:T(8,128)(2,1)S(1)} %collective-permute-done.1.refs_1_), channel_id=1, source_target_pairs={{0,16},{16,32},{32,48},{48,64},{64,80},{80,96},{96,112},{112,0},{1... | collective-permute-start | bytes 1179656 | tf_op jit(solution)/shard_map/ppermute | solution.py:337
  42.6 10.8 %collective-permute-start.4 = (bf16[256,768]{1,0:T(8,128)(2,1)S(1)}, bf16[256,768]{1,0:T(8,128)(2,1)S(1)}, u32[]{:S(2)}, u32[]{:S(2)}) collective-permute-start(bf16[256,768]{1,0:T(8,128)(2,1)S(1)} %collective-permute-done.2.refs_2_), channel_id=1, source_target_pairs={{0,112},{16,0},{32,16},{48,32},{64,48},{80,64},{96,80},{112,96},{1... | collective-permute-start | bytes 1179656 | tf_op jit(solution)/shard_map/ppermute | solution.py:337
  53.4 4.6 %copy-start.8 = (bf16[256,768]{1,0:T(8,128)(2,1)}, bf16[256,768]{1,0:T(8,128)(2,1)S(1)}, u32[]{:S(2)}) copy-start(bf16[256,768]{1,0:T(8,128)(2,1)S(1)} %collective-permute-done.3.refs_0_) | copy-start | bytes 1179652
  53.4 4.6 %copy-start.9 = (bf16[256,768]{1,0:T(8,128)(2,1)}, bf16[256,768]{1,0:T(8,128)(2,1)S(1)}, u32[]{:S(2)}) copy-start(bf16[256,768]{1,0:T(8,128)(2,1)S(1)} %collective-permute-done.4.refs_1_) | copy-start | bytes 1179652
  53.4 10.0 %collective-permute-start.5 = (bf16[256,768]{1,0:T(8,128)(2,1)S(1)}, bf16[256,768]{1,0:T(8,128)(2,1)S(1)}, u32[]{:S(2)}, u32[]{:S(2)}) collective-permute-start(bf16[256,768]{1,0:T(8,128)(2,1)S(1)} %collective-permute-done.3.refs_0_), channel_id=1, source_target_pairs={{0,16},{16,32},{32,48},{48,64},{64,80},{80,96},{96,112},{112,0},{1... | collective-permute-start | bytes 1179656 | tf_op jit(solution)/shard_map/ppermute | solution.py:337
  53.5 9.9 %collective-permute-start.6 = (bf16[256,768]{1,0:T(8,128)(2,1)S(1)}, bf16[256,768]{1,0:T(8,128)(2,1)S(1)}, u32[]{:S(2)}, u32[]{:S(2)}) collective-permute-start(bf16[256,768]{1,0:T(8,128)(2,1)S(1)} %collective-permute-done.4.refs_1_), channel_id=1, source_target_pairs={{0,112},{16,0},{32,16},{48,32},{64,48},{80,64},{96,80},{112,96},{1... | collective-permute-start | bytes 1179656 | tf_op jit(solution)/shard_map/ppermute | solution.py:337
  63.4 4.9 %copy-start.3 = (bf16[256,768]{1,0:T(8,128)(2,1)}, bf16[256,768]{1,0:T(8,128)(2,1)S(1)}, u32[]{:S(2)}) copy-start(bf16[256,768]{1,0:T(8,128)(2,1)S(1)} %collective-permute-done.5.refs_0_) | copy-start | bytes 1179652
  63.4 4.9 %copy-start.4 = (bf16[256,768]{1,0:T(8,128)(2,1)}, bf16[256,768]{1,0:T(8,128)(2,1)S(1)}, u32[]{:S(2)}) copy-start(bf16[256,768]{1,0:T(8,128)(2,1)S(1)} %collective-permute-done.6.refs_1_) | copy-start | bytes 1179652
  63.4 9.7 %collective-permute-start.7 = (bf16[128,768]{1,0:T(8,128)(2,1)S(1)}, bf16[128,768]{1,0:T(8,128)(2,1)S(1)}, u32[]{:S(2)}, u32[]{:S(2)}) collective-permute-start(bf16[128,768]{1,0:T(8,128)(2,1)S(1)} %slice.6), channel_id=1, source_target_pairs={{0,16},{16,32},{32,48},{48,64},{64,80},{80,96},{96,112},{112,0},{1... | collective-permute-start | bytes 589832 | tf_op jit(solution)/shard_map/ppermute | solution.py:337
  65.4 7.7 %collective-permute-start.8 = (bf16[128,768]{1,0:T(8,128)(2,1)S(1)}, bf16[128,768]{1,0:T(8,128)(2,1)S(1)}, u32[]{:S(2)}, u32[]{:S(2)}) collective-permute-start(bf16[128,768]{1,0:T(8,128)(2,1)S(1)} %slice.7), channel_id=1, source_target_pairs={{0,112},{16,0},{32,16},{48,32},{64,48},{80,64},{96,80},{112,96},{1... | collective-permute-start | bytes 589832 | tf_op jit(solution)/shard_map/ppermute | solution.py:337
  73.1 0.7 copy-start.1
  73.8 0.7 copy-start.2
Sparse Core Ops, SparseCore 0:
  17.9 57.4 all-gather.1

commit v3 on v2

--- a/solution.py
+++ b/solution.py
@@ -23,20 +23,25 @@
     return pltpu.CompilerParams(vmem_limit_bytes=mib * MIB)
 
 
-def norm_kernel(x_ref, gain_ref, out_ref):
-    x = x_ref[...].astype(F32)
-    center = jnp.mean(x, axis=-1, keepdims=True)
-    d = x - center
-    spread = jnp.mean(d * d, axis=-1, keepdims=True)
-    out_ref[...] = (d * lax.rsqrt(spread + EPS) * gain_ref[...]).astype(BF16)
-
-
-def norm_rows(x, gain):
+def norm_kernel(*refs):
+    gain_ref, out_ref = refs[-2:]
+    at = 0
+    for x_ref in refs[:-2]:
+        x = x_ref[...].astype(F32)
+        center = jnp.mean(x, axis=-1, keepdims=True)
+        d = x - center
+        spread = jnp.mean(d * d, axis=-1, keepdims=True)
+        out_ref[at : at + x.shape[0], :] = (d * lax.rsqrt(spread + EPS) * gain_ref[...]).astype(BF16)
+        at += x.shape[0]
+
+
+def norm_rows(parts, gain):
+    rows = sum(x.shape[0] for x in parts)
     return pl.pallas_call(
         norm_kernel,
-        out_shape=jax.ShapeDtypeStruct(x.shape, BF16),
+        out_shape=jax.ShapeDtypeStruct((rows, gain.shape[0]), BF16),
         compiler_params=params(61),
-    )(x, gain.reshape(1, -1))
+    )(*parts, gain.reshape(1, -1))
 
 
 def bias_kernel(step, pair_ref, gain_ref, proj_ref, out_ref, x_ref, sem, swap_ref):
@@ -82,7 +87,7 @@
 def pair_bias(pair, gain, proj_t):
     rows, nk, nc = pair.shape
     heads = proj_t.shape[0]
-    step = 16
+    step = 32
     vmem = pl.BlockSpec(memory_space=pltpu.VMEM)
     return pl.pallas_call(
         functools.partial(bias_kernel, step),
@@ -96,7 +101,7 @@
         ],
         compiler_params=params(61),
         cost_estimate=pl.CostEstimate(
-            flops=rows * nk * nc * 400, bytes_accessed=rows * nk * nc * 2, transcendentals=0
+            flops=rows * nk * nc * 400, bytes_accessed=28 * MIB, transcendentals=0
         ),
     )(pair, gain.reshape(1, -1), proj_t)
 
@@ -144,7 +149,7 @@
 
 
 def prepare(x, w, chain_index, chain_query, key_mask, chain_gain):
-    n, width = x.shape
+    n, width = chain_query.shape[0], x.shape[1]
     heads = chain_gain.shape[0]
     keys = chain_index.shape[0]
     pairs, depth = heads // 2, 128
@@ -251,31 +256,28 @@
     fetch(q_hbm, q_ref, 0).wait()
     fetch(limit_hbm, limit_ref, 1).wait()
 
-    def scores(i):
-        g, c0 = i // per, i % per * lanes
+    def await_keys(i):
+        g = i // per
         if i % per == 0:
             for copy in fetch_keys(g):
                 copy.wait()
             fetch(bias_ref.at[:, g * per * lanes : (g + 1) * per * lanes], b_ref.at[g], bias_sem(g)).wait()
-        top = None
-        for c in range(tokens // n):
-            s = dot(k_ref[c * n : (c + 1) * n, i * depth : (i + 1) * depth], q_ref[i], ((1,), (0,)))
-            mask = limit_ref[pl.ds(pl.multiple_of(pos_ref[c] * n, n), n), :]
-            s = s + b_ref[g, c * n : (c + 1) * n, c0 : c0 + lanes].astype(F32)
-            s = jnp.minimum(s, jnp.concatenate([mask, mask], axis=1))
-            s_ref[i % 2, c * n : (c + 1) * n, :] = s
-            t = jnp.max(s.reshape(n // 8, 8, lanes), axis=0)
-            top = t if top is None else jnp.maximum(top, t)
-        return jnp.max(top, axis=0, keepdims=True)
-
-    def soften(i, top):
-        total = None
-        for c in range(tokens // n):
-            p = jnp.exp2(s_ref[i % 2, c * n : (c + 1) * n, :] - top)
-            p_ref[i % 2, c * n : (c + 1) * n, :] = p.astype(BF16)
-            t = jnp.sum(p.reshape(n // 8, 8, lanes), axis=0)
-            total = t if total is None else total + t
-        return jnp.sum(total, axis=0, keepdims=True)
+
+    def score(i, c, top):
+        g, c0 = i // per, i % per * lanes
+        s = dot(k_ref[c * n : (c + 1) * n, i * depth : (i + 1) * depth], q_ref[i], ((1,), (0,)))
+        limit = limit_ref[pl.ds(pl.multiple_of(pos_ref[c] * n, n), n), :]
+        s = s + b_ref[g, c * n : (c + 1) * n, c0 : c0 + lanes].astype(F32)
+        s = jnp.minimum(s, jnp.concatenate([limit, limit], axis=1))
+        s_ref[i % 2, c * n : (c + 1) * n, :] = s
+        t = jnp.max(s.reshape(n // 8, 8, lanes), axis=0)
+        return t if top is None else jnp.maximum(top, t)
+
+    def soften(i, c, top, total):
+        p = jnp.exp2(s_ref[i % 2, c * n : (c + 1) * n, :] - top)
+        p_ref[i % 2, c * n : (c + 1) * n, :] = p.astype(BF16)
+        t = jnp.sum(p.reshape(n // 8, 8, lanes), axis=0)
+        return t if total is None else total + t
 
     def weigh(i, total):
         rows = slice(2 * i * hdim, (2 * i + 2) * hdim)
@@ -288,12 +290,22 @@
         o = jnp.concatenate([o[:hdim, :nq], o[hdim:, nq:]], axis=0)
         hid_ref[rows, :] = (gate_ref[rows, :] * o).astype(BF16)
 
-    top = scores(0)
+    chunks = range(tokens // n)
+    await_keys(0)
+    top = None
+    for c in chunks:
+        top = score(0, c, top)
     for i in range(pairs):
-        total = soften(i, top)
         if i + 1 < pairs:
-            top = scores(i + 1)
-        weigh(i, total)
+            await_keys(i + 1)
+        top = jnp.max(top, axis=0, keepdims=True)
+        total = after = None
+        for c in chunks:
+            if i + 1 < pairs:
+                after = score(i + 1, c, after)
+            total = soften(i, c, top, total)
+        top = after
+        weigh(i, jnp.sum(total, axis=0, keepdims=True))
 
     fetch(w_hbm, w_ref, 3).wait()
     out_ref[...] = dot(hid_ref[...], w_ref[...], ((0,), (0,))).astype(BF16)
@@ -341,11 +353,10 @@
     return lax.ppermute(x, "pb", [(i, (i + 8) % 16) for i in range(16)])
 
 
-def attended_rows(own, prepared, bias, w_out):
+def attended_rows(both, prepared, bias, w_out):
     me = lax.axis_index("pb")
     y, z = me // 8, me % 8
-    n = own.shape[0]
-    both = jnp.concatenate([own, swap_y(own)], axis=0)
+    n = both.shape[0] // 2
 
     def places(by):
         return [y * 8 + (z + by) % 8, (1 - y) * 8 + (z + by) % 8]
@@ -377,10 +388,11 @@
 def body(tokens, pair, token_chain_index, key_mask, norm_gain, pair_gain, pair_proj, chain_gain, w_qkvg, w_out):
     nq = tokens.shape[1]
 
-    normed = norm_rows(tokens[0], norm_gain)
-    tile, normed = lax.optimization_barrier((pair, normed))
-    bias = pair_bias(tile, pair_gain, pair_proj.T)
+    other = swap_y(tokens[0])
+    bias = pair_bias(pair, pair_gain, pair_proj.T)
+    other, bias = lax.optimization_barrier((other, bias))
     bias_all = lax.all_gather(bias, "ka", axis=0, tiled=True)
+    normed = norm_rows([tokens[0], other], norm_gain)
     chain_query = lax.dynamic_slice_in_dim(token_chain_index, lax.axis_index("pb") * nq, nq)
     prepared = prepare(normed, w_qkvg, token_chain_index, chain_query, key_mask, chain_gain)
     return attended_rows(normed, prepared, bias_all, w_out)[None]

time: 96.9 us -> 92.6 us (0.956)
  waiting for transfers between devices: 6.36 us -> 2.72 us
    ppermute x1, waiting for transfers between devices: 4.93 us -> 0.01 us  [swap_y(): return lax.ppermute(x, 'pb', [(i, (i + 8) % 16) for i in range(16)])]
    ppermute x8, waiting for transfers between devices: 1.4 us -> 2.69 us  [shift_z(): return lax.ppermute(x, 'pb', [(i, to(i)) for i in range(16)])]
  transfers between devices with their start and end apart: 10 -> 10, of which waited for: 3 -> 2; matrix products, arithmetic and copies ran while one was open for 7% -> 8% of each run, Pallas kernels for 27% -> 40%
where the time goes in v3:
time: 92.6 us; the launch traced here: 91.7 us
  Pallas kernels  47.7 us (52%)
  starting transfers between devices  19.3 us (21%)
  between operations  13.5 us (15%)
  local copies, waits for them, and re-layouts  6.61 us (7%)
  waiting for transfers between devices  2.72 us (3%)
  other arithmetic  1.84 us (2%)
    pallas_call x4, Pallas kernels, keys_values(): pl.pallas_call(functools.partial(kv_kernel, tokens // pos.shape[0]), in_s...  19.5 us
    ppermute x8, starting transfers between devices, shift_z(): return lax.ppermute(x, 'pb', [(i, to(i)) for i in range(16)])  16.1 us
    pallas_call x1, Pallas kernels, attend(): pl.pallas_call(functools.partial(attend_kernel, tokens // pos.shape[0], l...  11.4 us
    pallas_call x1, Pallas kernels, pair_bias(): pl.pallas_call(functools.partial(bias_kernel, step), in_specs=[pl.BlockSp...  7.46 us
    pallas_call x1, Pallas kernels, prepare(): pl.pallas_call(prepare_kernel, grid=(1,), in_specs=[whole(n, width)] + [p...  7.25 us
    ppermute x1, starting transfers between devices, swap_y(): return lax.ppermute(x, 'pb', [(i, (i + 8) % 16) for i in range(16)])  3.19 us
    ppermute x8, waiting for transfers between devices, shift_z(): return lax.ppermute(x, 'pb', [(i, to(i)) for i in range(16)])  2.69 us
    pallas_call x1, Pallas kernels, norm_rows(): pl.pallas_call(norm_kernel, out_shape=jax.ShapeDtypeStruct((rows, gain.sh...  2.07 us
  transfers between devices with their start and end apart: 10, of which 2 were waited for; matrix products, arithmetic and copies ran while one was open for 8% of the time, Pallas kernels for 40%

profile of v3, /device:TPU:2, one launch (start us, length us, event | category | flops | bytes accessed | tf_op | source)
XLA Modules:
  0.0 91.7 jit_solution(6248288717815631872)
XLA Ops:
  6.5 3.2 %collective-permute-start = (bf16[128,768]{1,0:T(8,128)(2,1)}, bf16[128,768]{1,0:T(8,128)(2,1)S(1)}, u32[]{:S(2)}, u32[]{:S(2)}) collective-permute-start(bf16[128,768]{1,0:T(8,128)(2,1)} %bitcast.24), channel_id=1, source_target_pairs={{0,128},{16,144},{32,160},{48,176},{64,192},{80,208},{96,224},{112... | collective-permute-start | bytes 589832 | tf_op jit(solution)/shard_map/ppermute | solution.py:353
  9.7 7.5 %shard_map.100 = bf16[128,2048]{1,0:T(8,128)(2,1)} custom-call(bf16[128,128,128]{2,1,0:T(8,128)(2,1)} %pair_ref.1, f32[1,128]{1,0:T(1,128)} %bitcast.29, f32[16,128]{1,0:T(8,128)} %bitcast.26), custom_call_target="tpu_custom_call" | custom-call | flops 838860800 | bytes 29360128 | tf_op jit(solution)/shard_map/pallas_call | solution.py:92
  17.3 0.6 reshape.16.refs_2_
  17.9 2.1 %shard_map.101.x_ref.refs_0_ = bf16[256,768]{1,0:T(8,128)(2,1)} custom-call(bf16[128,768]{1,0:T(8,128)(2,1)} %bitcast.25, bf16[128,768]{1,0:T(8,128)(2,1)} %copy-done, f32[1,768]{1,0:T(1,128)} %reshape.16.refs_2_), custom_call_target="tpu_custom_call" | custom-call | tf_op jit(solution)/shard_map/pallas_call | solution.py:40
  20.0 1.9 %collective-permute-start.1 = (bf16[256,768]{1,0:T(8,128)(2,1)}, bf16[256,768]{1,0:T(8,128)(2,1)S(1)}, u32[]{:S(2)}, u32[]{:S(2)}) collective-permute-start(bf16[256,768]{1,0:T(8,128)(2,1)} %shard_map.101.x_ref.refs_0_), channel_id=1, source_target_pairs={{0,16},{16,32},{32,48},{48,64},{64,80},{80,96},{96,112},{112,0},{1... | collective-permute-start | bytes 1179656 | tf_op jit(solution)/shard_map/ppermute | solution.py:349
  21.9 3.9 %collective-permute-start.2 = (bf16[256,768]{1,0:T(8,128)(2,1)}, bf16[256,768]{1,0:T(8,128)(2,1)S(1)}, u32[]{:S(2)}, u32[]{:S(2)}) collective-permute-start(bf16[256,768]{1,0:T(8,128)(2,1)} %shard_map.101.x_ref.refs_0_), channel_id=1, source_target_pairs={{0,112},{16,0},{32,16},{48,32},{64,48},{80,64},{96,80},{112,96},{1... | collective-permute-start | bytes 1179656 | tf_op jit(solution)/shard_map/ppermute | solution.py:349
  25.8 1.4 %copy.11.chain_ref = s32[2048,1]{1,0:T(8,128)} copy(s32[2048,1]{0,1:T(1,128)S(1)} %bitcast.28) | data formatting | bytes 16384 | tf_op jit(solution)/shard_map/reshape | solution.py:174
  27.2 1.3 %copy.12.mask_ref = s32[2048,1]{1,0:T(8,128)} copy(s32[2048,1]{0,1:T(1,128)S(1)} %bitcast.27) | data formatting | bytes 16384 | tf_op jit(solution)/shard_map/reshape | solution.py:174
  29.1 7.3 %shard_map.102 = (bf16[8,128,256]{2,1,0:T(8,128)(2,1)}, f32[768,128]{1,0:T(8,128)}, bf16[768,1024]{1,0:T(8,128)(2,1)}, bf16[768,768]{1,0:T(8,128)(2,1)}, bf16[2048,128]{1,0:T(8,128)(2,1)}, /*index=5*/f32[2048,128]{1,0:T(8,128)}) custom-call(bf16[256,768]{1,0:T(8,128)(2,1)} %shard_map.101.x_ref.refs_0_, bf16[768,3072]{1,0:T(8,128)(2,1)} %wg_ref.1, ...), custom_call_target="tpu_custom_call" | custom-call | flops 603979776 | bytes 12582912 | tf_op jit(solution)/shard_map/pallas_call | solution.py:164
  36.5 3.2 %collective-permute-start.4 = (bf16[256,768]{1,0:T(8,128)(2,1)S(1)}, bf16[256,768]{1,0:T(8,128)(2,1)S(1)}, u32[]{:S(2)}, u32[]{:S(2)}) collective-permute-start(bf16[256,768]{1,0:T(8,128)(2,1)S(1)} %collective-permute-done.2.refs_2_), channel_id=1, source_target_pairs={{0,112},{16,0},{32,16},{48,32},{64,48},{80,64},{96,80},{112,96},{1... | collective-permute-start | bytes 1179656 | tf_op jit(solution)/shard_map/ppermute | solution.py:349
  39.7 0.7 stack.76.pos_ref
  40.4 6.2 %shard_map.103 = (bf16[768,1024]{1,0:T(8,128)(2,1)}, bf16[768,768]{1,0:T(8,128)(2,1)}) custom-call(s32[6]{0:T(128)} %stack.76.pos_ref, bf16[768,1024]{1,0:T(8,128)(2,1)} %get-tuple-element.50.wide_ref, bf16[768,768]{1,0:T(8,128)(2,1)} %get-tuple-element.51.turned_ref, bf16[2048,128]{1,0:T(8,128)(2,1)} %get-tuple-element.52.hot_ref, ...), custom_call_target="tpu_custom_call" | custom-call | flops 2264924160 | bytes 8388608 | tf_op jit(solution)/shard_map/pallas_call | solution.py:196
  46.6 1.4 %collective-permute-done.3.refs_0_ = bf16[256,768]{1,0:T(8,128)(2,1)S(1)} collective-permute-done((bf16[256,768]{1,0:T(8,128)(2,1)S(1)}, bf16[256,768]{1,0:T(8,128)(2,1)S(1)}, u32[]{:S(2)}, u32[]{:S(2)}) %collective-permute-start.3) | collective-permute-done | bytes 393248 | tf_op jit(solution)/shard_map/ppermute | solution.py:349
  48.1 3.2 %collective-permute-start.6 = (bf16[256,768]{1,0:T(8,128)(2,1)S(1)}, bf16[256,768]{1,0:T(8,128)(2,1)S(1)}, u32[]{:S(2)}, u32[]{:S(2)}) collective-permute-start(bf16[256,768]{1,0:T(8,128)(2,1)S(1)} %collective-permute-done.4.refs_1_), channel_id=1, source_target_pairs={{0,112},{16,0},{32,16},{48,32},{64,48},{80,64},{96,80},{112,96},{1... | collective-permute-start | bytes 1179656 | tf_op jit(solution)/shard_map/ppermute | solution.py:349
  51.3 0.7 pad_add_fusion.2.pos_ref
  52.6 4.8 %shard_map.104 = (bf16[512,1024]{1,0:T(8,128)(2,1)}, bf16[768,512]{1,0:T(8,128)(2,1)}) custom-call(s32[4]{0:T(128)} %pad_add_fusion.pos_ref, bf16[768,1024]{1,0:T(8,128)(2,1)} %get-tuple-element.50.wide_ref, bf16[768,768]{1,0:T(8,128)(2,1)} %get-tuple-element.51.turned_ref, bf16[2048,128]{1,0:T(8,128)(2,1)} %get-tuple-element.52.hot_ref, ...), custom_call_target="tpu_custom_call" | custom-call | flops 1509949440 | bytes 8388608 | tf_op jit(solution)/shard_map/pallas_call | solution.py:196
  57.4 1.3 %collective-permute-done.5.refs_0_ = bf16[256,768]{1,0:T(8,128)(2,1)S(1)} collective-permute-done((bf16[256,768]{1,0:T(8,128)(2,1)S(1)}, bf16[256,768]{1,0:T(8,128)(2,1)S(1)}, u32[]{:S(2)}, u32[]{:S(2)}) %collective-permute-start.5) | collective-permute-done | bytes 393248 | tf_op jit(solution)/shard_map/ppermute | solution.py:349
  58.7 1.2 %collective-permute-start.7 = (bf16[128,768]{1,0:T(8,128)(2,1)S(1)}, bf16[128,768]{1,0:T(8,128)(2,1)S(1)}, u32[]{:S(2)}, u32[]{:S(2)}) collective-permute-start(bf16[128,768]{1,0:T(8,128)(2,1)S(1)} %slice.6), channel_id=1, source_target_pairs={{0,16},{16,32},{32,48},{48,64},{64,80},{80,96},{96,112},{112,0},{1... | collective-permute-start | bytes 589832 | tf_op jit(solution)/shard_map/ppermute | solution.py:349
  59.9 2.4 %collective-permute-start.8 = (bf16[128,768]{1,0:T(8,128)(2,1)S(1)}, bf16[128,768]{1,0:T(8,128)(2,1)S(1)}, u32[]{:S(2)}, u32[]{:S(2)}) collective-permute-start(bf16[128,768]{1,0:T(8,128)(2,1)S(1)} %slice.7), channel_id=1, source_target_pairs={{0,112},{16,0},{32,16},{48,32},{64,48},{80,64},{96,80},{112,96},{1... | collective-permute-start | bytes 589832 | tf_op jit(solution)/shard_map/ppermute | solution.py:349
  63.5 4.8 %shard_map.105 = (bf16[512,1024]{1,0:T(8,128)(2,1)}, bf16[768,512]{1,0:T(8,128)(2,1)}) custom-call(s32[4]{0:T(128)} %pad_add_fusion.1.pos_ref, bf16[768,1024]{1,0:T(8,128)(2,1)} %get-tuple-element.50.wide_ref, bf16[768,768]{1,0:T(8,128)(2,1)} %get-tuple-element.51.turned_ref, bf16[2048,128]{1,0:T(8,128)(2,1)} %get-tuple-element.52.hot_ref, ...), custom_call_target="tpu_custom_call" | custom-call | flops 1509949440 | bytes 8388608 | tf_op jit(solution)/shard_map/pallas_call | solution.py:196
  68.3 0.7 copy-done.1
  69.0 0.7 copy-done.2
  69.7 3.7 %shard_map.106 = (bf16[256,1024]{1,0:T(8,128)(2,1)}, bf16[768,256]{1,0:T(8,128)(2,1)}) custom-call(s32[2]{0:T(128)} %pad_add_fusion.2.pos_ref, bf16[768,1024]{1,0:T(8,128)(2,1)} %get-tuple-element.50.wide_ref, bf16[768,768]{1,0:T(8,128)(2,1)} %get-tuple-element.51.turned_ref, bf16[2048,128]{1,0:T(8,128)(2,1)} %get-tuple-element.52.hot_ref, ...), custom_call_target="tpu_custom_call" | custom-call | flops 754974720 | bytes 8388608 | tf_op jit(solution)/shard_map/pallas_call | solution.py:196
  73.4 11.4 %shard_map.107 = bf16[128,768]{1,0:T(8,128)(2,1)} custom-call(s32[16]{0:T(128)} %concatenate.4.pos_ref, bf16[8,128,256]{2,1,0:T(8,128)(2,1)} %get-tuple-element.44.q_hbm, bf16[2048,2048]{1,0:T(8,128)(2,1)} %all-gather.2.cloned.1.call-done.bias_ref, f32[2048,128]{1,0:T(8,128)} %get-tuple-element.46.limit_hbm, f32[768,128]{1,0:T(8,128)} %get-tuple-element.47.gate_hbm, ...), custom_call_target="tpu_custom_call" | custom-call | flops 4294967296 | bytes 8388608 | tf_op jit(solution)/shard_map/pallas_call | solution.py:320
  (40 shorter events, 2.7 us)
Async XLA Ops:
  6.5 66.9 %all-gather.2.cloned.1.call-start = ((), (), s32[]{:S(2)}) async-start(), calls=%async_computation | async-start | bytes 8912896 | tf_op jit(solution)/shard_map/all_gather | solution.py:394
  6.5 10.7 %collective-permute-start = (bf16[128,768]{1,0:T(8,128)(2,1)}, bf16[128,768]{1,0:T(8,128)(2,1)S(1)}, u32[]{:S(2)}, u32[]{:S(2)}) collective-permute-start(bf16[128,768]{1,0:T(8,128)(2,1)} %bitcast.24), channel_id=1, source_target_pairs={{0,128},{16,144},{32,160},{48,176},{64,192},{80,208},{96,224},{112... | collective-permute-start | bytes 589832 | tf_op jit(solution)/shard_map/ppermute | solution.py:353
  9.7 7.5 %copy-start.7 = (f32[768]{0:T(1024)S(1)}, f32[768]{0:T(1024)}, u32[]{:S(2)}) copy-start(f32[768]{0:T(1024)} %param.14) | copy-start | bytes 9220
  9.7 16.1 %copy-start.6 = (s32[2048]{0:T(1024)S(1)}, s32[2048]{0:T(1024)}, u32[]{:S(2)}) copy-start(s32[2048]{0:T(1024)} %param.12) | copy-start | bytes 24580
  17.2 10.0 %copy-start.5 = (s32[2048]{0:T(1024)S(1)}, s32[2048]{0:T(1024)}, u32[]{:S(2)}) copy-start(s32[2048]{0:T(1024)} %param.13) | copy-start | bytes 24580
  17.2 0.7 copy-start
  20.0 16.4 %collective-permute-start.1 = (bf16[256,768]{1,0:T(8,128)(2,1)}, bf16[256,768]{1,0:T(8,128)(2,1)S(1)}, u32[]{:S(2)}, u32[]{:S(2)}) collective-permute-start(bf16[256,768]{1,0:T(8,128)(2,1)} %shard_map.101.x_ref.refs_0_), channel_id=1, source_target_pairs={{0,16},{16,32},{32,48},{48,64},{64,80},{80,96},{96,112},{112,0},{1... | collective-permute-start | bytes 1179656 | tf_op jit(solution)/shard_map/ppermute | solution.py:349
  21.9 14.5 %collective-permute-start.2 = (bf16[256,768]{1,0:T(8,128)(2,1)}, bf16[256,768]{1,0:T(8,128)(2,1)S(1)}, u32[]{:S(2)}, u32[]{:S(2)}) collective-permute-start(bf16[256,768]{1,0:T(8,128)(2,1)} %shard_map.101.x_ref.refs_0_), channel_id=1, source_target_pairs={{0,112},{16,0},{32,16},{48,32},{64,48},{80,64},{96,80},{112,96},{1... | collective-permute-start | bytes 1179656 | tf_op jit(solution)/shard_map/ppermute | solution.py:349
  36.4 4.0 %copy-start.10 = (bf16[256,768]{1,0:T(8,128)(2,1)}, bf16[256,768]{1,0:T(8,128)(2,1)S(1)}, u32[]{:S(2)}) copy-start(bf16[256,768]{1,0:T(8,128)(2,1)S(1)} %collective-permute-done.1.refs_1_) | copy-start | bytes 1179652
  36.4 4.0 %copy-start.11 = (bf16[256,768]{1,0:T(8,128)(2,1)}, bf16[256,768]{1,0:T(8,128)(2,1)S(1)}, u32[]{:S(2)}) copy-start(bf16[256,768]{1,0:T(8,128)(2,1)S(1)} %collective-permute-done.2.refs_2_) | copy-start | bytes 1179652
  36.4 11.6 %collective-permute-start.3 = (bf16[256,768]{1,0:T(8,128)(2,1)S(1)}, bf16[256,768]{1,0:T(8,128)(2,1)S(1)}, u32[]{:S(2)}, u32[]{:S(2)}) collective-permute-start(bf16[256,768]{1,0:T(8,128)(2,1)S(1)} %collective-permute-done.1.refs_1_), channel_id=1, source_target_pairs={{0,16},{16,32},{32,48},{48,64},{64,80},{80,96},{96,112},{112,0},{1... | collective-permute-start | bytes 1179656 | tf_op jit(solution)/shard_map/ppermute | solution.py:349
  36.5 11.5 %collective-permute-start.4 = (bf16[256,768]{1,0:T(8,128)(2,1)S(1)}, bf16[256,768]{1,0:T(8,128)(2,1)S(1)}, u32[]{:S(2)}, u32[]{:S(2)}) collective-permute-start(bf16[256,768]{1,0:T(8,128)(2,1)S(1)} %collective-permute-done.2.refs_2_), channel_id=1, source_target_pairs={{0,112},{16,0},{32,16},{48,32},{64,48},{80,64},{96,80},{112,96},{1... | collective-permute-start | bytes 1179656 | tf_op jit(solution)/shard_map/ppermute | solution.py:349
  48.0 4.6 %copy-start.8 = (bf16[256,768]{1,0:T(8,128)(2,1)}, bf16[256,768]{1,0:T(8,128)(2,1)S(1)}, u32[]{:S(2)}) copy-start(bf16[256,768]{1,0:T(8,128)(2,1)S(1)} %collective-permute-done.3.refs_0_) | copy-start | bytes 1179652
  48.0 4.6 %copy-start.9 = (bf16[256,768]{1,0:T(8,128)(2,1)}, bf16[256,768]{1,0:T(8,128)(2,1)S(1)}, u32[]{:S(2)}) copy-start(bf16[256,768]{1,0:T(8,128)(2,1)S(1)} %collective-permute-done.4.refs_1_) | copy-start | bytes 1179652
  48.0 10.7 %collective-permute-start.5 = (bf16[256,768]{1,0:T(8,128)(2,1)S(1)}, bf16[256,768]{1,0:T(8,128)(2,1)S(1)}, u32[]{:S(2)}, u32[]{:S(2)}) collective-permute-start(bf16[256,768]{1,0:T(8,128)(2,1)S(1)} %collective-permute-done.3.refs_0_), channel_id=1, source_target_pairs={{0,16},{16,32},{32,48},{48,64},{64,80},{80,96},{96,112},{112,0},{1... | collective-permute-start | bytes 1179656 | tf_op jit(solution)/shard_map/ppermute | solution.py:349
  48.1 10.6 %collective-permute-start.6 = (bf16[256,768]{1,0:T(8,128)(2,1)S(1)}, bf16[256,768]{1,0:T(8,128)(2,1)S(1)}, u32[]{:S(2)}, u32[]{:S(2)}) collective-permute-start(bf16[256,768]{1,0:T(8,128)(2,1)S(1)} %collective-permute-done.4.refs_1_), channel_id=1, source_target_pairs={{0,112},{16,0},{32,16},{48,32},{64,48},{80,64},{96,80},{112,96},{1... | collective-permute-start | bytes 1179656 | tf_op jit(solution)/shard_map/ppermute | solution.py:349
  58.7 4.9 %copy-start.3 = (bf16[256,768]{1,0:T(8,128)(2,1)}, bf16[256,768]{1,0:T(8,128)(2,1)S(1)}, u32[]{:S(2)}) copy-start(bf16[256,768]{1,0:T(8,128)(2,1)S(1)} %collective-permute-done.5.refs_0_) | copy-start | bytes 1179652
  58.7 4.9 %copy-start.4 = (bf16[256,768]{1,0:T(8,128)(2,1)}, bf16[256,768]{1,0:T(8,128)(2,1)S(1)}, u32[]{:S(2)}) copy-start(bf16[256,768]{1,0:T(8,128)(2,1)S(1)} %collective-permute-done.6.refs_1_) | copy-start | bytes 1179652
  58.7 9.6 %collective-permute-start.7 = (bf16[128,768]{1,0:T(8,128)(2,1)S(1)}, bf16[128,768]{1,0:T(8,128)(2,1)S(1)}, u32[]{:S(2)}, u32[]{:S(2)}) collective-permute-start(bf16[128,768]{1,0:T(8,128)(2,1)S(1)} %slice.6), channel_id=1, source_target_pairs={{0,16},{16,32},{32,48},{48,64},{64,80},{80,96},{96,112},{112,0},{1... | collective-permute-start | bytes 589832 | tf_op jit(solution)/shard_map/ppermute | solution.py:349
  59.9 8.4 %collective-permute-start.8 = (bf16[128,768]{1,0:T(8,128)(2,1)S(1)}, bf16[128,768]{1,0:T(8,128)(2,1)S(1)}, u32[]{:S(2)}, u32[]{:S(2)}) collective-permute-start(bf16[128,768]{1,0:T(8,128)(2,1)S(1)} %slice.7), channel_id=1, source_target_pairs={{0,112},{16,0},{32,16},{48,32},{64,48},{80,64},{96,80},{112,96},{1... | collective-permute-start | bytes 589832 | tf_op jit(solution)/shard_map/ppermute | solution.py:349
  68.3 0.7 copy-start.1
  69.0 0.7 copy-start.2
Sparse Core Ops, SparseCore 0:
  17.4 55.3 all-gather.1

commit v4 on v3

--- a/solution.py
+++ b/solution.py
@@ -139,13 +139,13 @@
     for i in range(pairs):
         wide_ref[:, i * depth : i * depth + 2 * hdim] = wk_ref[:, 2 * i * hdim : (2 * i + 2) * hdim]
     turned_ref[...] = wv_ref[...].T
-    step = 256
-    lane = lax.broadcasted_iota(jnp.int32, (step, depth), 1) - 2 * hdim
-    kind = jnp.where((lane >= 0) & (lane < 24), lane % 8, -1)
-    for c in range(0, chain_ref.shape[0], step):
-        hot_ref[c : c + step, :] = (chain_ref[c : c + step, :] == kind).astype(F32).astype(BF16)
-        keep = jnp.broadcast_to(mask_ref[c : c + step, :], (step, limit_ref.shape[1]))
-        limit_ref[c : c + step, :] = jnp.where(keep > 0, F32(3.0e38), F32(NEG))
+    lane = lax.broadcasted_iota(jnp.int32, (depth, depth), 1) - 2 * hdim
+    kind = jnp.where((lane >= 0) & (lane < 24), lane % 8, -1).astype(F32)
+    for c in range(0, chain_ref.shape[1], depth):
+        chain = jnp.broadcast_to(chain_ref[:, c : c + depth].astype(F32), (depth, depth)).T
+        hot_ref[c : c + depth, :] = (chain == kind).astype(F32).astype(BF16)
+        limit = jnp.where(mask_ref[:, c : c + depth] > 0, F32(3.0e38), F32(NEG))
+        limit_ref[c : c + depth, :] = jnp.broadcast_to(limit, (depth, depth)).T
 
 
 def prepare(x, w, chain_index, chain_query, key_mask, chain_gain):
@@ -159,19 +159,19 @@
         ((width, pairs * depth), BF16),
         ((width, width), BF16),
         ((keys, depth), BF16),
-        ((keys, n), F32),
+        ((keys, depth), F32),
     ]
     return pl.pallas_call(
         prepare_kernel,
         grid=(1,),
         in_specs=[whole(n, width)]
         + [pl.BlockSpec((width, width), lambda i, j=j: (0, j)) for j in range(4)]
-        + [whole(1, n), whole(keys, 1), whole(keys, 1), pl.BlockSpec(memory_space=pltpu.SMEM)],
+        + [whole(1, n), whole(1, keys), whole(1, keys), pl.BlockSpec(memory_space=pltpu.SMEM)],
         out_specs=[whole(*d) for d, _ in shapes],
         out_shape=[jax.ShapeDtypeStruct(d, t) for d, t in shapes],
         compiler_params=params(61),
         cost_estimate=pl.CostEstimate(flops=8 * n * width * width, bytes_accessed=12 * MIB, transcendentals=0),
-    )(x, w, w, w, w, chain_query.reshape(1, n), chain_index.reshape(keys, 1), key_mask.reshape(keys, 1), chain_gain)
+    )(x, w, w, w, w, chain_query.reshape(1, n), chain_index.reshape(1, keys), key_mask.reshape(1, keys), chain_gain)
 
 
 def kv_kernel(n, pos_ref, wide_ref, turned_ref, hot_ref, *refs):
@@ -213,8 +213,9 @@
     nq = lanes // 2
     tokens = limit_ref.shape[0]
     hdim = w_ref.shape[0] // (2 * pairs)
-    groups = b_ref.shape[0]
-    per = pairs // groups
+    runs = [(0, 1), (1, 2), (2, 4), (4, pairs)]
+    groups = len(runs)
+    first_of = {lo: g for g, (lo, _) in enumerate(runs)}
     starts = [0]
     for k in k_hbm:
         starts.append(starts[-1] + k.shape[0])
@@ -223,14 +224,14 @@
         return pltpu.make_async_copy(src, dst, sem.at[i])
 
     def fetch_keys(g):
-        cols = slice(g * per * depth, (g + 1) * per * depth)
+        cols = slice(runs[g][0] * depth, runs[g][1] * depth)
         return [
             fetch(k.at[:, cols], k_ref.at[starts[b] : starts[b + 1], cols], 4 + b * groups + g)
             for b, k in enumerate(k_hbm)
         ]
 
     def fetch_values(g):
-        rows = slice(2 * g * per * hdim, 2 * (g + 1) * per * hdim)
+        rows = slice(2 * runs[g][0] * hdim, 2 * runs[g][1] * hdim)
         return [
             fetch(v.at[rows, :], v_ref.at[rows, starts[b] : starts[b + 1]], 4 + (batches + b) * groups + g)
             for b, v in enumerate(v_hbm)
@@ -239,35 +240,42 @@
     def bias_sem(g):
         return 4 + 2 * batches * groups + g
 
+    def start_group(g):
+        for copy in fetch_keys(g):
+            copy.start()
+        cols = slice(runs[g][0] * lanes, runs[g][1] * lanes)
+        for c in range(tokens // n):
+            at = pl.multiple_of(pos_ref[c] * n, n)
+            fetch(bias_ref.at[pl.ds(at, n), cols], b_ref.at[pl.ds(c * n, n), cols], bias_sem(g)).start()
+        for copy in fetch_values(g):
+            copy.start()
+
     fetch(q_hbm, q_ref, 0).start()
     fetch(limit_hbm, limit_ref, 1).start()
-    for g in range(groups):
-        for copy in fetch_keys(g):
-            copy.start()
-        cols = slice(g * per * lanes, (g + 1) * per * lanes)
-        for c in range(tokens // n):
-            at = pl.multiple_of(pos_ref[c] * n, n)
-            fetch(bias_ref.at[pl.ds(at, n), cols], b_ref.at[g, pl.ds(c * n, n)], bias_sem(g)).start()
-        for copy in fetch_values(g):
-            copy.start()
-        if g == 0:
-            fetch(gate_hbm, gate_ref, 2).start()
+    start_group(0)
+    fetch(gate_hbm, gate_ref, 2).start()
+    for g in range(1, groups):
+        start_group(g)
     fetch(w_hbm, w_ref, 3).start()
     fetch(q_hbm, q_ref, 0).wait()
     fetch(limit_hbm, limit_ref, 1).wait()
 
+    wide = [None]
+
     def await_keys(i):
-        g = i // per
-        if i % per == 0:
+        g = first_of.get(i)
+        if g is not None:
             for copy in fetch_keys(g):
                 copy.wait()
-            fetch(bias_ref.at[:, g * per * lanes : (g + 1) * per * lanes], b_ref.at[g], bias_sem(g)).wait()
+            cols = slice(runs[g][0] * lanes, runs[g][1] * lanes)
+            fetch(bias_ref.at[:, cols], b_ref.at[:, cols], bias_sem(g)).wait()
 
     def score(i, c, top):
-        g, c0 = i // per, i % per * lanes
-        s = dot(k_ref[c * n : (c + 1) * n, i * depth : (i + 1) * depth], q_ref[i], ((1,), (0,)))
+        if c * n % 256 == 0:
+            wide[0] = dot(k_ref[c * n : c * n + 256, i * depth : (i + 1) * depth], q_ref[i], ((1,), (0,)))
+        s = wide[0][c * n % 256 : c * n % 256 + n]
         limit = limit_ref[pl.ds(pl.multiple_of(pos_ref[c] * n, n), n), :]
-        s = s + b_ref[g, c * n : (c + 1) * n, c0 : c0 + lanes].astype(F32)
+        s = s + b_ref[c * n : (c + 1) * n, i * lanes : (i + 1) * lanes].astype(F32)
         s = jnp.minimum(s, jnp.concatenate([limit, limit], axis=1))
         s_ref[i % 2, c * n : (c + 1) * n, :] = s
         t = jnp.max(s.reshape(n // 8, 8, lanes), axis=0)
@@ -283,8 +291,8 @@
         rows = slice(2 * i * hdim, (2 * i + 2) * hdim)
         if i == 0:
             fetch(gate_hbm, gate_ref, 2).wait()
-        if i % per == 0:
-            for copy in fetch_values(i // per):
+        if i in first_of:
+            for copy in fetch_values(first_of[i]):
                 copy.wait()
         o = dot(v_ref[rows, :], p_ref[i % 2], ((1,), (0,))) / total
         o = jnp.concatenate([o[:hdim, :nq], o[hdim:, nq:]], axis=0)
@@ -329,7 +337,7 @@
             pltpu.VMEM(w_out.shape, BF16),
             pltpu.VMEM((tokens, ks[0].shape[1]), BF16),
             pltpu.VMEM((width, tokens), BF16),
-            pltpu.VMEM((groups, tokens, pairs // groups * lanes), BF16),
+            pltpu.VMEM((tokens, pairs * lanes), BF16),
             pltpu.SemaphoreType.DMA((4 + (2 * len(ks) + 1) * groups,)),
             pltpu.VMEM((width, nq), BF16),
             pltpu.VMEM((2, tokens, lanes), F32),

time: 92.6 us -> 92.3 us (level)
  waiting for transfers between devices: 2.72 us -> 4.96 us
  local copies, waits for them, and re-layouts: 6.61 us -> 4.53 us
  Pallas kernels: 47.7 us -> 46.5 us
    reshape x2 -> x0, local copies, waits for them, and re-layouts: 2.71 us -> none  [the longest x1 1.37 us: prepare(): chain_index.reshape(keys, 1)]
    all_gather x1, waiting for transfers between devices: 0.01 us -> 1.44 us  [body(): bias_all = lax.all_gather(bias, 'ka', axis=0, tiled=True)]
  transfers between devices with their start and end apart: 10 -> 10, of which waited for: 2 -> 4; matrix products, arithmetic and copies ran while one was open for 8% -> 5% of each run, Pallas kernels for 40% -> 39%
where the time goes in v4:
time: 92.3 us; the launch traced here: 90.7 us
  Pallas kernels  46.5 us (50%)
  starting transfers between devices  19.5 us (21%)
  between operations  13.5 us (15%)
  waiting for transfers between devices  4.96 us (5%)
  local copies, waits for them, and re-layouts  4.53 us (5%)
  other arithmetic  1.82 us (2%)
    pallas_call x4, Pallas kernels, keys_values(): pl.pallas_call(functools.partial(kv_kernel, tokens // pos.shape[0]), in_s...  19.4 us
    ppermute x8, starting transfers between devices, shift_z(): return lax.ppermute(x, 'pb', [(i, to(i)) for i in range(16)])  16.3 us
    pallas_call x1, Pallas kernels, attend(): pl.pallas_call(functools.partial(attend_kernel, tokens // pos.shape[0], l...  11.1 us
    pallas_call x1, Pallas kernels, pair_bias(): pl.pallas_call(functools.partial(bias_kernel, step), in_specs=[pl.BlockSp...  7.43 us
    pallas_call x1, Pallas kernels, prepare(): pl.pallas_call(prepare_kernel, grid=(1,), in_specs=[whole(n, width)] + [p...  6.42 us
    ppermute x8, waiting for transfers between devices, shift_z(): return lax.ppermute(x, 'pb', [(i, to(i)) for i in range(16)])  3.49 us
    ppermute x1, starting transfers between devices, swap_y(): return lax.ppermute(x, 'pb', [(i, (i + 8) % 16) for i in range(16)])  3.19 us
    pallas_call x1, Pallas kernels, norm_rows(): pl.pallas_call(norm_kernel, out_shape=jax.ShapeDtypeStruct((rows, gain.sh...  2.06 us
  transfers between devices with their start and end apart: 10, of which 4 were waited for; matrix products, arithmetic and copies ran while one was open for 5% of the time, Pallas kernels for 39%

profile of v4, /device:TPU:2, one launch (start us, length us, event | category | flops | bytes accessed | tf_op | source)
XLA Modules:
  0.0 90.7 jit_solution(12193101984790975673)
XLA Ops:
  6.5 3.2 %collective-permute-start = (bf16[128,768]{1,0:T(8,128)(2,1)}, bf16[128,768]{1,0:T(8,128)(2,1)S(1)}, u32[]{:S(2)}, u32[]{:S(2)}) collective-permute-start(bf16[128,768]{1,0:T(8,128)(2,1)} %bitcast.24), channel_id=1, source_target_pairs={{0,128},{16,144},{32,160},{48,176},{64,192},{80,208},{96,224},{112... | collective-permute-start | bytes 589832 | tf_op jit(solution)/shard_map/ppermute | solution.py:361
  9.7 7.4 %shard_map.100 = bf16[128,2048]{1,0:T(8,128)(2,1)} custom-call(bf16[128,128,128]{2,1,0:T(8,128)(2,1)} %pair_ref.1, f32[1,128]{1,0:T(1,128)} %bitcast.29, f32[16,128]{1,0:T(8,128)} %bitcast.26), custom_call_target="tpu_custom_call" | custom-call | flops 838860800 | bytes 29360128 | tf_op jit(solution)/shard_map/pallas_call | solution.py:92
  17.9 2.1 %shard_map.101.x_ref.refs_0_ = bf16[256,768]{1,0:T(8,128)(2,1)} custom-call(bf16[128,768]{1,0:T(8,128)(2,1)} %bitcast.25, bf16[128,768]{1,0:T(8,128)(2,1)} %copy-done, f32[1,768]{1,0:T(1,128)} %reshape.16.refs_2_), custom_call_target="tpu_custom_call" | custom-call | tf_op jit(solution)/shard_map/pallas_call | solution.py:40
  19.9 1.9 %collective-permute-start.1 = (bf16[256,768]{1,0:T(8,128)(2,1)}, bf16[256,768]{1,0:T(8,128)(2,1)S(1)}, u32[]{:S(2)}, u32[]{:S(2)}) collective-permute-start(bf16[256,768]{1,0:T(8,128)(2,1)} %shard_map.101.x_ref.refs_0_), channel_id=1, source_target_pairs={{0,16},{16,32},{32,48},{48,64},{64,80},{80,96},{96,112},{112,0},{1... | collective-permute-start | bytes 1179656 | tf_op jit(solution)/shard_map/ppermute | solution.py:357
  21.8 3.9 %collective-permute-start.2 = (bf16[256,768]{1,0:T(8,128)(2,1)}, bf16[256,768]{1,0:T(8,128)(2,1)S(1)}, u32[]{:S(2)}, u32[]{:S(2)}) collective-permute-start(bf16[256,768]{1,0:T(8,128)(2,1)} %shard_map.101.x_ref.refs_0_), channel_id=1, source_target_pairs={{0,112},{16,0},{32,16},{48,32},{64,48},{80,64},{96,80},{112,96},{1... | collective-permute-start | bytes 1179656 | tf_op jit(solution)/shard_map/ppermute | solution.py:357
  25.8 1.3 %dynamic-slice_bitcast_fusion.chain_row_ref = s32[1,128]{1,0:T(1,128)} fusion(s32[2048]{0:T(1024)} %param.12, s32[]{:T(128)S(6)} %select_n.72), kind=kLoop, calls=%fused_computation.3 | loop fusion | bytes 1028 | tf_op jit(solution)/shard_map/reshape | solution.py:174
  27.1 6.4 %shard_map.102 = (bf16[8,128,256]{2,1,0:T(8,128)(2,1)}, f32[768,128]{1,0:T(8,128)}, bf16[768,1024]{1,0:T(8,128)(2,1)}, bf16[768,768]{1,0:T(8,128)(2,1)}, bf16[2048,128]{1,0:T(8,128)(2,1)}, /*index=5*/f32[2048,128]{1,0:T(8,128)}) custom-call(bf16[256,768]{1,0:T(8,128)(2,1)} %shard_map.101.x_ref.refs_0_, bf16[768,3072]{1,0:T(8,128)(2,1)} %wg_ref.1, ...), custom_call_target="tpu_custom_call" | custom-call | flops 603979776 | bytes 12582912 | tf_op jit(solution)/shard_map/pallas_call | solution.py:164
  33.5 1.3 %collective-permute-done.1.refs_1_ = bf16[256,768]{1,0:T(8,128)(2,1)S(1)} collective-permute-done((bf16[256,768]{1,0:T(8,128)(2,1)}, bf16[256,768]{1,0:T(8,128)(2,1)S(1)}, u32[]{:S(2)}, u32[]{:S(2)}) %collective-permute-start.1) | collective-permute-done | bytes 393248 | tf_op jit(solution)/shard_map/ppermute | solution.py:357
  34.9 3.2 %collective-permute-start.4 = (bf16[256,768]{1,0:T(8,128)(2,1)S(1)}, bf16[256,768]{1,0:T(8,128)(2,1)S(1)}, u32[]{:S(2)}, u32[]{:S(2)}) collective-permute-start(bf16[256,768]{1,0:T(8,128)(2,1)S(1)} %collective-permute-done.2.refs_2_), channel_id=1, source_target_pairs={{0,112},{16,0},{32,16},{48,32},{64,48},{80,64},{96,80},{112,96},{1... | collective-permute-start | bytes 1179656 | tf_op jit(solution)/shard_map/ppermute | solution.py:357
  38.8 6.2 %shard_map.103 = (bf16[768,1024]{1,0:T(8,128)(2,1)}, bf16[768,768]{1,0:T(8,128)(2,1)}) custom-call(s32[6]{0:T(128)} %stack.76.pos_ref, bf16[768,1024]{1,0:T(8,128)(2,1)} %get-tuple-element.50.wide_ref, bf16[768,768]{1,0:T(8,128)(2,1)} %get-tuple-element.51.turned_ref, bf16[2048,128]{1,0:T(8,128)(2,1)} %get-tuple-element.52.hot_ref, ...), custom_call_target="tpu_custom_call" | custom-call | flops 2264924160 | bytes 8388608 | tf_op jit(solution)/shard_map/pallas_call | solution.py:196
  44.9 1.2 %collective-permute-done.3.refs_0_ = bf16[256,768]{1,0:T(8,128)(2,1)S(1)} collective-permute-done((bf16[256,768]{1,0:T(8,128)(2,1)S(1)}, bf16[256,768]{1,0:T(8,128)(2,1)S(1)}, u32[]{:S(2)}, u32[]{:S(2)}) %collective-permute-start.3) | collective-permute-done | bytes 393248 | tf_op jit(solution)/shard_map/ppermute | solution.py:357
  46.1 1.8 %collective-permute-start.5 = (bf16[256,768]{1,0:T(8,128)(2,1)S(1)}, bf16[256,768]{1,0:T(8,128)(2,1)S(1)}, u32[]{:S(2)}, u32[]{:S(2)}) collective-permute-start(bf16[256,768]{1,0:T(8,128)(2,1)S(1)} %collective-permute-done.3.refs_0_), channel_id=1, source_target_pairs={{0,16},{16,32},{32,48},{48,64},{64,80},{80,96},{96,112},{112,0},{1... | collective-permute-start | bytes 1179656 | tf_op jit(solution)/shard_map/ppermute | solution.py:357
  47.9 1.7 %collective-permute-start.6 = (bf16[256,768]{1,0:T(8,128)(2,1)S(1)}, bf16[256,768]{1,0:T(8,128)(2,1)S(1)}, u32[]{:S(2)}, u32[]{:S(2)}) collective-permute-start(bf16[256,768]{1,0:T(8,128)(2,1)S(1)} %collective-permute-done.4.refs_1_), channel_id=1, source_target_pairs={{0,112},{16,0},{32,16},{48,32},{64,48},{80,64},{96,80},{112,96},{1... | collective-permute-start | bytes 1179656 | tf_op jit(solution)/shard_map/ppermute | solution.py:357
  49.6 0.7 pad_add_fusion.2.pos_ref
  50.8 4.8 %shard_map.104 = (bf16[512,1024]{1,0:T(8,128)(2,1)}, bf16[768,512]{1,0:T(8,128)(2,1)}) custom-call(s32[4]{0:T(128)} %pad_add_fusion.pos_ref, bf16[768,1024]{1,0:T(8,128)(2,1)} %get-tuple-element.50.wide_ref, bf16[768,768]{1,0:T(8,128)(2,1)} %get-tuple-element.51.turned_ref, bf16[2048,128]{1,0:T(8,128)(2,1)} %get-tuple-element.52.hot_ref, ...), custom_call_target="tpu_custom_call" | custom-call | flops 1509949440 | bytes 8388608 | tf_op jit(solution)/shard_map/pallas_call | solution.py:196
  55.7 1.0 %collective-permute-done.5.refs_0_ = bf16[256,768]{1,0:T(8,128)(2,1)S(1)} collective-permute-done((bf16[256,768]{1,0:T(8,128)(2,1)S(1)}, bf16[256,768]{1,0:T(8,128)(2,1)S(1)}, u32[]{:S(2)}, u32[]{:S(2)}) %collective-permute-start.5) | collective-permute-done | bytes 393248 | tf_op jit(solution)/shard_map/ppermute | solution.py:357
  56.6 1.4 %collective-permute-start.7 = (bf16[128,768]{1,0:T(8,128)(2,1)S(1)}, bf16[128,768]{1,0:T(8,128)(2,1)S(1)}, u32[]{:S(2)}, u32[]{:S(2)}) collective-permute-start(bf16[128,768]{1,0:T(8,128)(2,1)S(1)} %slice.6), channel_id=1, source_target_pairs={{0,16},{16,32},{32,48},{48,64},{64,80},{80,96},{96,112},{112,0},{1... | collective-permute-start | bytes 589832 | tf_op jit(solution)/shard_map/ppermute | solution.py:357
  58.0 2.2 %collective-permute-start.8 = (bf16[128,768]{1,0:T(8,128)(2,1)S(1)}, bf16[128,768]{1,0:T(8,128)(2,1)S(1)}, u32[]{:S(2)}, u32[]{:S(2)}) collective-permute-start(bf16[128,768]{1,0:T(8,128)(2,1)S(1)} %slice.7), channel_id=1, source_target_pairs={{0,112},{16,0},{32,16},{48,32},{64,48},{80,64},{96,80},{112,96},{1... | collective-permute-start | bytes 589832 | tf_op jit(solution)/shard_map/ppermute | solution.py:357
  61.5 4.8 %shard_map.105 = (bf16[512,1024]{1,0:T(8,128)(2,1)}, bf16[768,512]{1,0:T(8,128)(2,1)}) custom-call(s32[4]{0:T(128)} %pad_add_fusion.1.pos_ref, bf16[768,1024]{1,0:T(8,128)(2,1)} %get-tuple-element.50.wide_ref, bf16[768,768]{1,0:T(8,128)(2,1)} %get-tuple-element.51.turned_ref, bf16[2048,128]{1,0:T(8,128)(2,1)} %get-tuple-element.52.hot_ref, ...), custom_call_target="tpu_custom_call" | custom-call | flops 1509949440 | bytes 8388608 | tf_op jit(solution)/shard_map/pallas_call | solution.py:196
  66.3 0.7 copy-done.1
  67.0 0.7 copy-done.2
  67.7 3.6 %shard_map.106 = (bf16[256,1024]{1,0:T(8,128)(2,1)}, bf16[768,256]{1,0:T(8,128)(2,1)}) custom-call(s32[2]{0:T(128)} %pad_add_fusion.2.pos_ref, bf16[768,1024]{1,0:T(8,128)(2,1)} %get-tuple-element.50.wide_ref, bf16[768,768]{1,0:T(8,128)(2,1)} %get-tuple-element.51.turned_ref, bf16[2048,128]{1,0:T(8,128)(2,1)} %get-tuple-element.52.hot_ref, ...), custom_call_target="tpu_custom_call" | custom-call | flops 754974720 | bytes 8388608 | tf_op jit(solution)/shard_map/pallas_call | solution.py:196
  71.3 1.4 %all-gather.2.cloned.1.call-done.bias_ref = bf16[2048,2048]{1,0:T(8,128)(2,1)} async-done(((bf16[128,2048]{1,0:T(8,128)(2,1)}), bf16[2048,2048]{1,0:T(8,128)(2,1)}) %all-gather.2.cloned.1.call-update) | async-done | bytes 8388624 | tf_op jit(solution)/shard_map/all_gather | solution.py:402
  72.7 11.1 %shard_map.107 = bf16[128,768]{1,0:T(8,128)(2,1)} custom-call(s32[16]{0:T(128)} %concatenate.4.pos_ref, bf16[8,128,256]{2,1,0:T(8,128)(2,1)} %get-tuple-element.44.q_hbm, bf16[2048,2048]{1,0:T(8,128)(2,1)} %all-gather.2.cloned.1.call-done.bias_ref, f32[2048,128]{1,0:T(8,128)} %get-tuple-element.46.limit_hbm, f32[768,128]{1,0:T(8,128)} %get-tuple-element.47.gate_hbm, ...), custom_call_target="tpu_custom_call" | custom-call | flops 4294967296 | bytes 8388608 | tf_op jit(solution)/shard_map/pallas_call | solution.py:328
  (34 shorter events, 3.2 us)
Async XLA Ops:
  6.5 66.2 %all-gather.2.cloned.1.call-start = ((), (), s32[]{:S(2)}) async-start(), calls=%async_computation | async-start | bytes 8912896 | tf_op jit(solution)/shard_map/all_gather | solution.py:402
  6.5 10.6 %collective-permute-start = (bf16[128,768]{1,0:T(8,128)(2,1)}, bf16[128,768]{1,0:T(8,128)(2,1)S(1)}, u32[]{:S(2)}, u32[]{:S(2)}) collective-permute-start(bf16[128,768]{1,0:T(8,128)(2,1)} %bitcast.24), channel_id=1, source_target_pairs={{0,128},{16,144},{32,160},{48,176},{64,192},{80,208},{96,224},{112... | collective-permute-start | bytes 589832 | tf_op jit(solution)/shard_map/ppermute | solution.py:361
  9.7 7.5 %copy-start.5 = (f32[768]{0:T(1024)S(1)}, f32[768]{0:T(1024)}, u32[]{:S(2)}) copy-start(f32[768]{0:T(1024)} %param.14) | copy-start | bytes 9220
  17.2 0.7 copy-start
  19.9 14.9 %collective-permute-start.1 = (bf16[256,768]{1,0:T(8,128)(2,1)}, bf16[256,768]{1,0:T(8,128)(2,1)S(1)}, u32[]{:S(2)}, u32[]{:S(2)}) collective-permute-start(bf16[256,768]{1,0:T(8,128)(2,1)} %shard_map.101.x_ref.refs_0_), channel_id=1, source_target_pairs={{0,16},{16,32},{32,48},{48,64},{64,80},{80,96},{96,112},{112,0},{1... | collective-permute-start | bytes 1179656 | tf_op jit(solution)/shard_map/ppermute | solution.py:357
  21.8 13.0 %collective-permute-start.2 = (bf16[256,768]{1,0:T(8,128)(2,1)}, bf16[256,768]{1,0:T(8,128)(2,1)S(1)}, u32[]{:S(2)}, u32[]{:S(2)}) collective-permute-start(bf16[256,768]{1,0:T(8,128)(2,1)} %shard_map.101.x_ref.refs_0_), channel_id=1, source_target_pairs={{0,112},{16,0},{32,16},{48,32},{64,48},{80,64},{96,80},{112,96},{1... | collective-permute-start | bytes 1179656 | tf_op jit(solution)/shard_map/ppermute | solution.py:357
  34.8 3.9 %copy-start.8 = (bf16[256,768]{1,0:T(8,128)(2,1)}, bf16[256,768]{1,0:T(8,128)(2,1)S(1)}, u32[]{:S(2)}) copy-start(bf16[256,768]{1,0:T(8,128)(2,1)S(1)} %collective-permute-done.1.refs_1_) | copy-start | bytes 1179652
  34.8 3.9 %copy-start.9 = (bf16[256,768]{1,0:T(8,128)(2,1)}, bf16[256,768]{1,0:T(8,128)(2,1)S(1)}, u32[]{:S(2)}) copy-start(bf16[256,768]{1,0:T(8,128)(2,1)S(1)} %collective-permute-done.2.refs_2_) | copy-start | bytes 1179652
  34.8 11.3 %collective-permute-start.3 = (bf16[256,768]{1,0:T(8,128)(2,1)S(1)}, bf16[256,768]{1,0:T(8,128)(2,1)S(1)}, u32[]{:S(2)}, u32[]{:S(2)}) collective-permute-start(bf16[256,768]{1,0:T(8,128)(2,1)S(1)} %collective-permute-done.1.refs_1_), channel_id=1, source_target_pairs={{0,16},{16,32},{32,48},{48,64},{64,80},{80,96},{96,112},{112,0},{1... | collective-permute-start | bytes 1179656 | tf_op jit(solution)/shard_map/ppermute | solution.py:357
  34.9 11.2 %collective-permute-start.4 = (bf16[256,768]{1,0:T(8,128)(2,1)S(1)}, bf16[256,768]{1,0:T(8,128)(2,1)S(1)}, u32[]{:S(2)}, u32[]{:S(2)}) collective-permute-start(bf16[256,768]{1,0:T(8,128)(2,1)S(1)} %collective-permute-done.2.refs_2_), channel_id=1, source_target_pairs={{0,112},{16,0},{32,16},{48,32},{64,48},{80,64},{96,80},{112,96},{1... | collective-permute-start | bytes 1179656 | tf_op jit(solution)/shard_map/ppermute | solution.py:357
  46.1 4.7 %copy-start.6 = (bf16[256,768]{1,0:T(8,128)(2,1)}, bf16[256,768]{1,0:T(8,128)(2,1)S(1)}, u32[]{:S(2)}) copy-start(bf16[256,768]{1,0:T(8,128)(2,1)S(1)} %collective-permute-done.3.refs_0_) | copy-start | bytes 1179652
  46.1 4.7 %copy-start.7 = (bf16[256,768]{1,0:T(8,128)(2,1)}, bf16[256,768]{1,0:T(8,128)(2,1)S(1)}, u32[]{:S(2)}) copy-start(bf16[256,768]{1,0:T(8,128)(2,1)S(1)} %collective-permute-done.4.refs_1_) | copy-start | bytes 1179652
  46.1 10.5 %collective-permute-start.5 = (bf16[256,768]{1,0:T(8,128)(2,1)S(1)}, bf16[256,768]{1,0:T(8,128)(2,1)S(1)}, u32[]{:S(2)}, u32[]{:S(2)}) collective-permute-start(bf16[256,768]{1,0:T(8,128)(2,1)S(1)} %collective-permute-done.3.refs_0_), channel_id=1, source_target_pairs={{0,16},{16,32},{32,48},{48,64},{64,80},{80,96},{96,112},{112,0},{1... | collective-permute-start | bytes 1179656 | tf_op jit(solution)/shard_map/ppermute | solution.py:357
  47.9 8.7 %collective-permute-start.6 = (bf16[256,768]{1,0:T(8,128)(2,1)S(1)}, bf16[256,768]{1,0:T(8,128)(2,1)S(1)}, u32[]{:S(2)}, u32[]{:S(2)}) collective-permute-start(bf16[256,768]{1,0:T(8,128)(2,1)S(1)} %collective-permute-done.4.refs_1_), channel_id=1, source_target_pairs={{0,112},{16,0},{32,16},{48,32},{64,48},{80,64},{96,80},{112,96},{1... | collective-permute-start | bytes 1179656 | tf_op jit(solution)/shard_map/ppermute | solution.py:357
  56.6 4.9 %copy-start.3 = (bf16[256,768]{1,0:T(8,128)(2,1)}, bf16[256,768]{1,0:T(8,128)(2,1)S(1)}, u32[]{:S(2)}) copy-start(bf16[256,768]{1,0:T(8,128)(2,1)S(1)} %collective-permute-done.5.refs_0_) | copy-start | bytes 1179652
  56.6 4.8 %copy-start.4 = (bf16[256,768]{1,0:T(8,128)(2,1)}, bf16[256,768]{1,0:T(8,128)(2,1)S(1)}, u32[]{:S(2)}) copy-start(bf16[256,768]{1,0:T(8,128)(2,1)S(1)} %collective-permute-done.6.refs_1_) | copy-start | bytes 1179652
  56.6 9.6 %collective-permute-start.7 = (bf16[128,768]{1,0:T(8,128)(2,1)S(1)}, bf16[128,768]{1,0:T(8,128)(2,1)S(1)}, u32[]{:S(2)}, u32[]{:S(2)}) collective-permute-start(bf16[128,768]{1,0:T(8,128)(2,1)S(1)} %slice.6), channel_id=1, source_target_pairs={{0,16},{16,32},{32,48},{48,64},{64,80},{80,96},{96,112},{112,0},{1... | collective-permute-start | bytes 589832 | tf_op jit(solution)/shard_map/ppermute | solution.py:357
  58.0 8.3 %collective-permute-start.8 = (bf16[128,768]{1,0:T(8,128)(2,1)S(1)}, bf16[128,768]{1,0:T(8,128)(2,1)S(1)}, u32[]{:S(2)}, u32[]{:S(2)}) collective-permute-start(bf16[128,768]{1,0:T(8,128)(2,1)S(1)} %slice.7), channel_id=1, source_target_pairs={{0,112},{16,0},{32,16},{48,32},{64,48},{80,64},{96,80},{112,96},{1... | collective-permute-start | bytes 589832 | tf_op jit(solution)/shard_map/ppermute | solution.py:357
  66.3 0.7 copy-start.1
  67.0 0.7 copy-start.2
Sparse Core Ops, SparseCore 0:
  17.3 55.3 all-gather.1
